TPU v7x, 256 devices: a whole 4x4x8 slice. The times are simulated.
256 devices in a mesh: dist: 64 (over z, y, core), rep: 4 (over x).
Axes of the slice: x: 4, y: 4, z: 8, core: 2. Of those that a mesh axis runs over, the one named last changes fastest.
Arguments:
- amplitudes: float32 [2816, 19200], P(None, 'dist'), may hold values from -6 to 6
- integrals: float32 [2816, 19200], P('dist', 'rep'), may hold values from -0.3125 to 0.3125
- slab_irrep: int32 [176], replicated, may hold values from 0 to 7, as said below
- virtual_irrep: int32 [1200], replicated, may hold values from 0 to 7, as said below
- occupied_irrep: int32 [16], replicated, may hold values from 0 to 7, as said below
- occupied_energy: float32 [16], replicated, may hold values from -2 to -0.5
- slab_energy: float32 [176], replicated, may hold values from 0.2 to 3
Outputs:
- update: float32 [2816, 2816], P('rep', 'dist')
Inputs may be any that keep to these rules, and one draw needn't show every extreme that they name: `slab_irrep`: labels do not fall along the slab; every one of the 8 irreps labels at least 11 slab orbitals. `virtual_irrep`: labels do not fall along the virtual orbitals; every one of the 8 irreps labels at least 75 virtual orbitals. `occupied_irrep`: every irrep labels exactly 2 occupied orbitals.
All inputs are finite; a program needn't handle non-finite values.
Results may differ from a plain program's by a relative error of at most 0.000084.
Values sent between devices are 32-bit elements; how exact they have to be, the bound alone decides.
A program may use at most 64 MiB of HBM per device.

v0:
```python
import jax
import jax.numpy as jnp
from jax import lax
from jax.sharding import PartitionSpec as P


def local(
    amplitudes, integrals, slab_irrep, virtual_irrep, occupied_irrep, occupied_energy, slab_energy
):
    rep_count = lax.axis_size("rep")
    rep_index = lax.axis_index("rep")
    dist_index = lax.axis_index("dist")
    total_rows = amplitudes.shape[0]
    my_rows = total_rows // rep_count
    pair_cols = amplitudes.shape[1]
    int_rows = integrals.shape[0]
    int_cols = integrals.shape[1]
    row_symmetry = jnp.bitwise_xor(slab_irrep[:, None], occupied_irrep[None, :]).reshape(-1)
    col_symmetry = jnp.bitwise_xor(virtual_irrep[:, None], occupied_irrep[None, :]).reshape(-1)
    amp_rows = lax.dynamic_slice_in_dim(amplitudes, rep_index * my_rows, my_rows, 0)
    amp_row_sym = lax.dynamic_slice_in_dim(row_symmetry, rep_index * my_rows, my_rows, 0)
    amp_col_sym = lax.dynamic_slice_in_dim(col_symmetry, dist_index * pair_cols, pair_cols, 0)
    amp_masked = jnp.where(amp_row_sym[:, None] == amp_col_sym[None, :], amp_rows, jnp.float32(0.0))
    int_row_sym = lax.dynamic_slice_in_dim(row_symmetry, dist_index * int_rows, int_rows, 0)
    int_col_sym = lax.dynamic_slice_in_dim(col_symmetry, rep_index * int_cols, int_cols, 0)
    int_masked = jnp.where(
        int_row_sym[:, None] == int_col_sym[None, :], integrals, jnp.float32(0.0)
    )
    whole_rows = lax.all_gather(int_masked, "rep", axis=1, tiled=True)
    int_blocks = lax.all_to_all(whole_rows, "dist", split_axis=1, concat_axis=0, tiled=True)
    partial_value = lax.dot_general(
        amp_masked,
        int_blocks,
        (((1,), (1,)), ((), ())),
        precision=lax.Precision.HIGHEST,
        preferred_element_type=jnp.float32,
    )
    cycle = lax.psum_scatter(partial_value, "dist", scatter_dimension=1, tiled=True)
    shifts = (occupied_energy[None, :] - slab_energy[:, None]).reshape(-1)
    row_shift = lax.dynamic_slice_in_dim(shifts, rep_index * my_rows, my_rows, 0)
    col_shift = lax.dynamic_slice_in_dim(shifts, dist_index * int_rows, int_rows, 0)
    return cycle / (row_shift[:, None] + col_shift[None, :])


def solution(mesh):
    return jax.shard_map(
        local,
        mesh=mesh,
        in_specs=(P(None, "dist"), P("dist", "rep"), P(), P(), P(), P(), P()),
        out_specs=P("rep", "dist"),
        check_vma=False,
    )
```

profile of v0, /device:TPU:1, one launch (start us, length us, event | category | flops | bytes accessed | tf_op | source)
XLA Modules:
  0.0 355.0 jit_solution(13706335026462985126)
XLA Ops:
  6.5 0.8 broadcast_xor_fusion.1
  7.4 0.9 broadcast_xor_fusion
  8.4 0.2 xor.41
  8.7 2.3 select_bitcast_fusion
  11.0 50.9 %all-gather.3.cloned.1.call-done = f32[4,4800,44]{1,2,0:T(8,128)} async-done(((f32[1,4800,44]{1,2,0:T(8,128)}), f32[4,4800,44]{1,2,0:T(8,128)}) %all-gather.3.cloned.1.call-update) | async-done | bytes 3379216 | tf_op jit(solution)/shard_map/all_gather | solution.py:29
  62.0 4.3 %copy.10 = f32[4,4800,44]{1,0,2:T(4,128)S(1)} copy(f32[4,4800,44]{1,2,0:T(8,128)} %all-gather.3.cloned.1.call-done) | data formatting | bytes 6758400 | tf_op jit(solution)/shard_map/all_gather | solution.py:29
  66.2 4.4 %reshape.27 = f32[19200,44]{0,1:T(8,128)} reshape(f32[4,4800,44]{1,0,2:T(4,128)S(1)} %copy.10) | data formatting | bytes 6758400
  70.7 7.1 %all_to_all.14 = f32[44,64,300]{2,1,0:T(8,128)} reshape(f32[44,19200]{1,0:T(8,128)} %bitcast.12) | data formatting | bytes 6758400 | tf_op jit(solution)/shard_map/all_to_all | solution.py:30
  77.8 6.9 %copy.11 = f32[44,64,300]{2,0,1:T(8,128)} copy(f32[44,64,300]{2,1,0:T(8,128)} %all_to_all.14) | data formatting | bytes 6758400 | tf_op jit(solution)/shard_map/all_to_all | solution.py:30
  84.7 10.9 %all-to-all-start = ((f32[44,64,300]{2,0,1:T(8,128)}), f32[44,64,300]{2,0,1:T(8,128)}, u32[]{:S(2)}, u32[]{:S(2)}) async-start(f32[44,64,300]{2,0,1:T(8,128)} %copy.11), calls=%async_computation | async-start | bytes 9437184 | tf_op jit(solution)/shard_map/all_to_all | solution.py:30
  95.7 105.3 %all-to-all-done = f32[44,64,300]{2,0,1:T(8,128)} async-done(((f32[44,64,300]{2,0,1:T(8,128)}), f32[44,64,300]{2,0,1:T(8,128)}, u32[]{:S(2)}, u32[]{:S(2)}) %all-to-all-start) | async-done | bytes 3379232 | tf_op jit(solution)/shard_map/all_to_all | solution.py:30
  201.0 5.0 %all_to_all.17 = f32[2816,300]{1,0:T(8,128)} reshape(f32[64,44,300]{2,1,0:T(8,128)} %bitcast.3) | data formatting | bytes 6758400 | tf_op jit(solution)/shard_map/all_to_all | solution.py:30
  206.0 18.1 %fusion.1 = f32[704,2816]{0,1:T(8,128)} fusion(f32[2816,300]{1,0:T(8,128)} %all_to_all.17, f32[2816,300]{0,1:T(8,128)} %param.7, s32[]{:T(128)S(6)} %select_n.23, s32[704]{0:T(1024)S(1)} %dynamic_slice.21, s32[300]{0:T(512)S(1)} %dynamic_slice.22), kind=kOutput, calls=%fused_computation.1 | convolution fusion | flops 7137292800 | bytes 13193140 | tf_op jit(solution)/shard_map/dot_general | solution.py:31
  224.2 98.0 %fusion = f32[704,48]{0,1:T(8,128)S(1)} fusion(f32[704,2816]{0,1:T(8,128)} %fusion.1), kind=kCustom, calls=%all-reduce-scatter | all-reduce-scatter fusion | flops 2162689 | bytes 8066048
  322.2 3.0 collective-permute-start.5
  325.3 3.3 collective-permute-start
  328.6 3.2 collective-permute-start.1
  331.8 3.5 collective-permute-start.2
  335.3 3.5 collective-permute-start.3
  338.8 3.9 %collective-permute-start.4 = (f32[704,48]{0,1:T(8,128)S(1)}, f32[704,48]{0,1:T(8,128)S(1)}, u32[]{:S(2)}, u32[]{:S(2)}) collective-permute-start(f32[704,48]{0,1:T(8,128)S(1)} %fusion), channel_id=1, source_target_pairs={{0,20},{4,24},{8,28},{12,32},{16,36},{20,40},{24,44},{28,48},{32,5... | collective-permute-start | bytes 405512
  343.1 0.6 dynamic-slice.4
  344.4 2.0 collective-permute-done.4
  346.4 1.1 concatenate
  347.4 0.8 dynamic-slice_divide_fusion
  (23 shorter events, 0.8 us)
Async XLA Ops:
  6.5 55.4 %all-gather.3.cloned.1.call-start = ((), (), s32[]{:S(2)}) async-start(), calls=%async_computation.1 | async-start | bytes 4669440 | tf_op jit(solution)/shard_map/all_gather | solution.py:29
  84.7 116.3 %all-to-all-start = ((f32[44,64,300]{2,0,1:T(8,128)}), f32[44,64,300]{2,0,1:T(8,128)}, u32[]{:S(2)}, u32[]{:S(2)}) async-start(f32[44,64,300]{2,0,1:T(8,128)} %copy.11), calls=%async_computation | async-start | bytes 9437184 | tf_op jit(solution)/shard_map/all_to_all | solution.py:30
  224.2 118.6 %copy-start = (f32[176]{0:T(256)S(1)}, f32[176]{0:T(256)}, u32[]{:S(2)}) copy-start(f32[176]{0:T(256)} %param.13) | copy-start | bytes 2116
  224.2 118.6 %copy-start.1 = (f32[16]{0:T(128)S(1)}, f32[16]{0:T(128)}, u32[]{:S(2)}) copy-start(f32[16]{0:T(128)} %param.12) | copy-start | bytes 196
  224.2 118.9 %copy-start.2 = (u32[256]{0:T(256)S(1)}, u32[256]{0:T(256)}, u32[]{:S(2)}) copy-start(u32[256]{0:T(256)} %constant.29) | copy-start | bytes 3076
  322.2 16.5 %collective-permute-start.5 = (f32[704,12]{0,1:T(8,128)S(1)}, f32[704,12]{0,1:T(8,128)S(1)}, u32[]{:S(2)}, u32[]{:S(2)}) collective-permute-start(f32[704,12]{0,1:T(8,128)S(1)} %slice), channel_id=1, source_target_pairs={{0,24},{4,28},{8,32},{12,36},{16,40},{20,44},{24,48},{28,52},{32,5... | collective-permute-start | bytes 101384
  325.3 19.1 %collective-permute-start = (f32[704,48]{0,1:T(8,128)S(1)}, f32[704,48]{0,1:T(8,128)S(1)}, u32[]{:S(2)}, u32[]{:S(2)}) collective-permute-start(f32[704,48]{0,1:T(8,128)S(1)} %fusion), channel_id=1, source_target_pairs={{0,4},{4,8},{8,12},{12,16},{16,20},{20,24},{24,28},{28,32},{32,36}... | collective-permute-start | bytes 405512
  328.6 15.8 %collective-permute-start.1 = (f32[704,48]{0,1:T(8,128)S(1)}, f32[704,48]{0,1:T(8,128)S(1)}, u32[]{:S(2)}, u32[]{:S(2)}) collective-permute-start(f32[704,48]{0,1:T(8,128)S(1)} %fusion), channel_id=1, source_target_pairs={{0,8},{4,12},{8,16},{12,20},{16,24},{20,28},{24,32},{28,36},{32,40... | collective-permute-start | bytes 405512
  331.8 12.6 %collective-permute-start.2 = (f32[704,48]{0,1:T(8,128)S(1)}, f32[704,48]{0,1:T(8,128)S(1)}, u32[]{:S(2)}, u32[]{:S(2)}) collective-permute-start(f32[704,48]{0,1:T(8,128)S(1)} %fusion), channel_id=1, source_target_pairs={{0,12},{4,16},{8,20},{12,24},{16,28},{20,32},{24,36},{28,40},{32,4... | collective-permute-start | bytes 405512
  335.3 9.1 %collective-permute-start.3 = (f32[704,48]{0,1:T(8,128)S(1)}, f32[704,48]{0,1:T(8,128)S(1)}, u32[]{:S(2)}, u32[]{:S(2)}) collective-permute-start(f32[704,48]{0,1:T(8,128)S(1)} %fusion), channel_id=1, source_target_pairs={{0,16},{4,20},{8,24},{12,28},{16,32},{20,36},{24,40},{28,44},{32,4... | collective-permute-start | bytes 405512
  338.8 7.6 %collective-permute-start.4 = (f32[704,48]{0,1:T(8,128)S(1)}, f32[704,48]{0,1:T(8,128)S(1)}, u32[]{:S(2)}, u32[]{:S(2)}) collective-permute-start(f32[704,48]{0,1:T(8,128)S(1)} %fusion), channel_id=1, source_target_pairs={{0,20},{4,24},{8,28},{12,32},{16,36},{20,40},{24,44},{28,48},{32,5... | collective-permute-start | bytes 405512
Sparse Core Ops, SparseCore 0:
  11.2 50.7 all-gather.2
where the time goes:
time: 357 us; the launch traced here: 355 us
  waiting for transfers between devices  158 us (44%)
  blocking collectives  98 us (27%)
  starting transfers between devices  31.3 us (9%)
  local copies, waits for them, and re-layouts  30.2 us (8%)
  matrix products  18.1 us (5%)
  between operations  14.2 us (4%)
  other arithmetic  4.84 us (1%)
    all_to_all x1, waiting for transfers between devices, local(): lax.all_to_all(whole_rows, 'dist', split_axis=1, concat_axis=0, tiled=True)  105 us
    unnamed x1, blocking collectives  98 us
    all_gather x1, waiting for transfers between devices, local(): whole_rows = lax.all_gather(int_masked, 'rep', axis=1, tiled=True)  50.9 us
    unnamed x6, starting transfers between devices  20.4 us
    all_to_all x3, local copies, waits for them, and re-layouts, local(): lax.all_to_all(whole_rows, 'dist', split_axis=1, concat_axis=0, tiled=True)  19 us
    dot_general x1, matrix products, local(): lax.dot_general(amp_masked, int_blocks, (((1,), (1,)), ((), ())), precisi...  18.1 us
    all_to_all x1, starting transfers between devices, local(): lax.all_to_all(whole_rows, 'dist', split_axis=1, concat_axis=0, tiled=True)  10.9 us
  transfers between devices with their start and end apart: 8, of which 3 were waited for; matrix products, arithmetic and copies ran while one was open for 0% of the time, Pallas kernels for 0%

commit v1 on v0

v1 whole, which is shorter than its diff:
```python
import jax
import jax.numpy as jnp
from jax import lax
from jax.experimental import pallas as pl
from jax.experimental.pallas import tpu as pltpu
from jax.sharding import PartitionSpec as P

MESH = pl.DeviceIdType.MESH
F32, BF16, I32 = jnp.float32, jnp.bfloat16, jnp.int32

O = 16
IRREPS = 8
Z, Y, X = 8, 4, 4
PLACES = 8
ROWS = 2816
COLS = 300
WIDE = 4800
HALF = 2400
BJ = 44
MY = 704
SLOTS = 40
QA = 88
APAD, BPAD = 304, 48
START = [(COLS * p) // O for p in range(PLACES)]


def halves(value):
    high = value.astype(BF16)
    return high, (value - high.astype(F32)).astype(BF16)


def matmul(left, right, dims):
    return lax.dot_general(left, right, (dims, ((), ())), preferred_element_type=F32)


NN = ((1,), (0,))
NT = ((1,), (1,))


def kernel(
    a_hbm,
    w_hbm,
    row_sym,
    a_col_sym,
    w_col_sym,
    bj_sym,
    a_code,
    bj_code,
    bj_code_col,
    rank_key,
    out_sym,
    out_shift,
    bj_shift,
    out_ref,
    a_in,
    w_in,
    a_split,
    w_split,
    pick,
    a_msg,
    w_msg,
    a_got,
    w_got,
    a_all,
    o_msg,
    o_got,
    load_sem,
    a_send,
    w_send,
    o_send,
    a_recv,
    w_recv,
    o_recv,
):
    d = lax.axis_index("dist")
    x = lax.axis_index("rep")
    z, place = d // PLACES, d % PLACES
    y, core = place // 2, place % 2
    home_y = (x - y + Y) % Y
    self_w = jnp.where((z // 2 == x) & (home_y == y), 1, 0)
    self_o = jnp.where(home_y == y, 1, 0)

    load_a = pltpu.make_async_copy(a_hbm, a_in, load_sem.at[0])
    load_w = pltpu.make_async_copy(w_hbm, w_in, load_sem.at[1])
    load_w.start()
    load_a.start()

    barrier = pltpu.get_barrier_semaphore()

    def greet(dd, xx):
        pl.semaphore_signal(barrier, inc=1, device_id=(dd, xx), device_id_type=MESH)

    def greet_a(i, carry):
        greet(z * PLACES + (place + i) % PLACES, x)
        return carry

    def greet_w(i, carry):
        zs = (z + i // 2) % Z
        cs = i % 2
        dd, xx = zs * PLACES + home_y * 2 + cs, z // 2

        @pl.when(jnp.logical_not((dd == d) & (xx == x)))
        def _():
            greet(dd, xx)

        return carry

    def greet_o(i, carry):
        zs = (z + i // PLACES) % Z
        s = (place + i) % PLACES
        dd, xx = zs * PLACES + s, (y + s // 2) % Y

        @pl.when(jnp.logical_not((dd == d) & (xx == x)))
        def _():
            greet(dd, xx)

        return carry

    lax.fori_loop(1, PLACES, greet_a, 0)
    lax.fori_loop(0, 2 * Z, greet_w, 0)
    lax.fori_loop(0, Z * PLACES, greet_o, 0)

    for n in range(8):
        cols = pl.ds(n * 256, 256)
        slot = lax.broadcasted_iota(I32, (256, 256), 0)
        pick[:, cols] = (rank_key[:, cols] == slot).astype(F32).astype(BF16)
    for n in range(4):
        o_msg[n] = jnp.zeros((2 * Z, 8, 128), F32)
        w_split[pl.ds(n * BPAD + 32, 16)] = jnp.zeros((16, 2432), BF16)
    for n in range(2):
        a_split[pl.ds(n * APAD + 288, 16)] = jnp.zeros((16, ROWS), BF16)

    load_w.wait()
    for half in range(2):
        cols = pl.ds(half * HALF, HALF)
        kept = jnp.where(bj_sym[pl.ds(0, BJ)] == w_col_sym[:, cols], w_in[:, cols], 0.0)
        high, low = halves(kept)
        w_split[pl.ds(half * 2 * BPAD, BJ), pl.ds(0, HALF)] = high
        w_split[pl.ds((half * 2 + 1) * BPAD, BJ), pl.ds(0, HALF)] = low
    w_main = matmul(w_split[:, pl.ds(0, 2048)], pick[...], NT)
    w_rest = matmul(
        w_split[:, pl.ds(2048, HALF - 2048)], pick[pl.ds(0, 128), pl.ds(0, HALF - 2048)], NT
    )
    group = lax.broadcasted_iota(I32, (IRREPS * 8, 2 * BPAD), 0) == bj_code[...]
    group = group.astype(F32).astype(BF16)
    for half in range(2):
        rows = slice(half * 2 * BPAD, (half + 1) * 2 * BPAD)
        main = matmul(group, w_main[rows].astype(BF16), NN)
        rest = matmul(group, w_rest[rows].astype(BF16), NN)
        w_msg[half, :, :, pl.ds(0, 256)] = main.reshape(IRREPS, 8, 256)
        w_msg[half, :, :, pl.ds(256, 128)] = rest.reshape(IRREPS, 8, 128)

    pl.semaphore_wait(barrier, 7 + 2 * Z - self_w + Z * PLACES - self_o)

    slot_w = z * 2 + core

    def w_route(i):
        half = i // PLACES
        s = (place + i) % PLACES
        dd, xx = (2 * x + half) * PLACES + s, (y + s // 2) % Y
        return half, s, dd, xx, (dd == d) & (xx == x)

    def w_copy(i):
        half, s, dd, xx, _ = w_route(i)
        return pltpu.make_async_remote_copy(
            src_ref=w_msg.at[half, s],
            dst_ref=w_got.at[slot_w],
            send_sem=w_send.at[i],
            recv_sem=w_recv,
            device_id=(dd, xx),
            device_id_type=MESH,
        )

    def send_w(i, carry):
        half, s, dd, xx, mine = w_route(i)

        @pl.when(mine)
        def _():
            pltpu.make_async_copy(w_msg.at[half, s], w_got.at[slot_w], w_recv).start()

        @pl.when(jnp.logical_not(mine))
        def _():
            w_copy(i).start()

        return carry

    lax.fori_loop(0, 2 * PLACES, send_w, 0)

    load_a.wait()
    for n in range(11):
        cols = pl.ds(n * 256, 256)
        kept = jnp.where(a_col_sym[...] == row_sym[:, cols], a_in[:, cols], 0.0)
        high, low = halves(kept)
        a_split[pl.ds(0, COLS), cols] = high
        a_split[pl.ds(APAD, COLS), cols] = low
    a_main = matmul(a_split[:, pl.ds(0, 2048)], pick[...], NT)
    a_rest = matmul(
        a_split[:, pl.ds(2048, ROWS - 2048)], pick[pl.ds(0, 128), pl.ds(0, ROWS - 2048)], NT
    )
    place_rows = lax.broadcasted_iota(I32, (IRREPS * SLOTS, 2 * APAD), 0) == a_code[...]
    place_rows = place_rows.astype(F32).astype(BF16)
    main = matmul(place_rows, a_main.astype(BF16), NN)
    rest = matmul(place_rows, a_rest.astype(BF16), NN)
    a_msg[:, :, pl.ds(0, 256)] = main.reshape(IRREPS, SLOTS, 256)
    a_msg[:, :, pl.ds(256, 128)] = rest.reshape(IRREPS, SLOTS, 128)

    def a_copy(i):
        s = (place + i) % PLACES
        return pltpu.make_async_remote_copy(
            src_ref=a_msg.at[s],
            dst_ref=a_got.at[place],
            send_sem=a_send.at[i],
            recv_sem=a_recv,
            device_id=(z * PLACES + s, x),
            device_id_type=MESH,
        )

    def send_a(i, carry):
        a_copy(i).start()
        return carry

    lax.fori_loop(1, PLACES, send_a, 0)
    pltpu.make_async_copy(a_msg.at[place], a_got.at[place], a_recv).start()

    a_all[...] = jnp.zeros(a_all.shape, F32)
    pltpu.make_async_copy(a_got, a_got, a_recv).wait()
    for p in range(PLACES):
        first = 2 * START[p]
        a_all[pl.ds(first, SLOTS), :] += a_got[p]
    pltpu.make_async_copy(w_got, w_got, w_recv).wait()
    w_high, w_low = halves(w_got[...].reshape(2 * Z * 8, 384))
    a_high, a_low = halves(a_all[...])
    product = matmul(w_high, a_low, NN) + matmul(w_low, a_high, NN)
    product = product + matmul(w_high, a_high, NN)
    for part in range(X):
        o_msg[part, :, :, pl.ds(0, QA)] = product[:, part * QA : (part + 1) * QA].reshape(
            2 * Z, 8, QA
        )

    def o_route(i):
        zs = (z + i // PLACES) % Z
        cs = (core + i) % 2
        part = (x + (i % PLACES) // 2) % X
        dd = zs * PLACES + home_y * 2 + cs
        return zs * 2 + cs, part, dd, (dd == d) & (part == x)

    def o_copy(i):
        w, part, dd, _ = o_route(i)
        return pltpu.make_async_remote_copy(
            src_ref=o_msg.at[part, w],
            dst_ref=o_got.at[d],
            send_sem=o_send.at[i],
            recv_sem=o_recv,
            device_id=(dd, part),
            device_id_type=MESH,
        )

    def send_o(i, carry):
        w, part, dd, mine = o_route(i)

        @pl.when(mine)
        def _():
            pltpu.make_async_copy(o_msg.at[part, w], o_got.at[d], o_recv).start()

        @pl.when(jnp.logical_not(mine))
        def _():
            o_copy(i).start()

        return carry

    lax.fori_loop(0, Z * PLACES, send_o, 0)

    spread = (
        lax.broadcasted_iota(I32, (BPAD, 128), 1) % 64 == bj_code_col[...]
    ).astype(F32).astype(BF16)
    pltpu.make_async_copy(o_got, o_got, o_recv).wait()
    total = o_got[pl.ds(0, PLACES)]
    for zs in range(1, Z):
        total = total + o_got[pl.ds(zs * PLACES, PLACES)]
    high, low = halves(total.reshape(IRREPS * 8, 128))
    mine = matmul(spread, jnp.concatenate([high, low], axis=0), NN)
    high, low = halves(mine)
    widen = pick[pl.ds(0, 128), pl.ds(0, MY)]
    cycle = matmul(high, widen, NN) + matmul(low, widen, NN)
    value = jnp.where(bj_sym[...] == out_sym[...], cycle, 0.0) / (out_shift[...] + bj_shift[...])
    out_ref[...] = value[:BJ]

    def done_w(i, carry):
        @pl.when(jnp.logical_not(w_route(i)[4]))
        def _():
            w_copy(i).wait_send()

        return carry

    def done_a(i, carry):
        a_copy(i).wait_send()
        return carry

    def done_o(i, carry):
        @pl.when(jnp.logical_not(o_route(i)[3]))
        def _():
            o_copy(i).wait_send()

        return carry

    lax.fori_loop(0, 2 * PLACES, done_w, 0)
    lax.fori_loop(1, PLACES, done_a, 0)
    lax.fori_loop(0, Z * PLACES, done_o, 0)


def local(
    amplitudes, integrals, slab_irrep, virtual_irrep, occupied_irrep, occupied_energy, slab_energy
):
    d = lax.axis_index("dist")
    x = lax.axis_index("rep")
    row_sym = (slab_irrep[:, None] ^ occupied_irrep[None, :]).reshape(-1)
    col_sym = (virtual_irrep[:, None] ^ occupied_irrep[None, :]).reshape(-1)
    shifts = (occupied_energy[None, :] - slab_energy[:, None]).reshape(-1)
    same = occupied_irrep[:, None] == occupied_irrep[None, :]
    earlier = jnp.arange(O)[None, :] < jnp.arange(O)[:, None]
    rank = jnp.sum((same & earlier).astype(I32), axis=1)

    a_sym = lax.dynamic_slice_in_dim(col_sym, d * COLS, COLS, 0)
    w_sym = lax.dynamic_slice_in_dim(col_sym, x * WIDE, WIDE, 0)
    bj_sym = lax.dynamic_slice_in_dim(row_sym, d * BJ, BJ, 0)
    out_sym = lax.dynamic_slice_in_dim(row_sym, x * MY, MY, 0)
    bj_shift = lax.dynamic_slice_in_dim(shifts, d * BJ, BJ, 0)
    out_shift = lax.dynamic_slice_in_dim(shifts, x * MY, MY, 0)

    position = (d % PLACES) * COLS + jnp.arange(COLS)
    ranks = jnp.tile(rank, 128)
    my_rank = lax.dynamic_slice_in_dim(jnp.tile(rank, 20), (d * COLS) % O, COLS, 0)
    a_slot = 2 * (position // O - ((d % PLACES) * COLS) // O) + my_rank
    a_code = SLOTS * a_sym + a_slot
    a_code = jnp.pad(a_code, (0, APAD - COLS), constant_values=-1)
    before = jnp.arange(BJ)[None, :] < jnp.arange(BJ)[:, None]
    bj_slot = jnp.sum(((bj_sym[:, None] == bj_sym[None, :]) & before).astype(I32), axis=1)
    bj_code = jnp.pad(8 * bj_sym + bj_slot, (0, BPAD - BJ), constant_values=-1)
    rank_key = 2 * (jnp.arange(2048) // O) + ranks

    def pad(v, size, value):
        return jnp.pad(v, (0, size - v.shape[0]), constant_values=value)

    vmem = pl.BlockSpec(memory_space=pltpu.VMEM)
    hbm = pl.BlockSpec(memory_space=pl.ANY)
    out = pl.pallas_call(
        kernel,
        out_shape=jax.ShapeDtypeStruct((BJ, MY), F32),
        in_specs=[hbm, hbm] + [vmem] * 11,
        out_specs=vmem,
        scratch_shapes=[
            pltpu.VMEM((COLS, ROWS), F32),
            pltpu.VMEM((BJ, WIDE), F32),
            pltpu.VMEM((2 * APAD, ROWS), BF16),
            pltpu.VMEM((4 * BPAD, 2432), BF16),
            pltpu.VMEM((256, 2048), BF16),
            pltpu.VMEM((IRREPS, SLOTS, 384), F32),
            pltpu.VMEM((2, IRREPS, 8, 384), F32),
            pltpu.VMEM((PLACES, SLOTS, 384), F32),
            pltpu.VMEM((2 * Z, 8, 384), F32),
            pltpu.VMEM((384, 384), F32),
            pltpu.VMEM((X, 2 * Z, 8, 128), F32),
            pltpu.VMEM((Z * PLACES, 8, 128), F32),
            pltpu.SemaphoreType.DMA((2,)),
            pltpu.SemaphoreType.DMA((PLACES,)),
            pltpu.SemaphoreType.DMA((2 * PLACES,)),
            pltpu.SemaphoreType.DMA((Z * PLACES,)),
            pltpu.SemaphoreType.DMA,
            pltpu.SemaphoreType.DMA,
            pltpu.SemaphoreType.DMA,
        ],
        compiler_params=pltpu.CompilerParams(
            collective_id=0, has_side_effects=True, vmem_limit_bytes=48 * 1024 * 1024
        ),
    )(
        amplitudes.T,
        integrals,
        row_sym[None, :],
        a_sym[:, None],
        w_sym[None, :],
        pad(bj_sym, BPAD, -1)[:, None],
        jnp.concatenate([a_code, a_code])[None, :],
        jnp.concatenate([bj_code, bj_code])[None, :],
        bj_code[:, None],
        rank_key[None, :],
        out_sym[None, :],
        out_shift[None, :],
        pad(bj_shift, BPAD, 1.0)[:, None],
    )
    return out.T


def solution(mesh):
    return jax.shard_map(
        local,
        mesh=mesh,
        in_specs=(P(None, "dist"), P("dist", "rep"), P(), P(), P(), P(), P()),
        out_specs=P("rep", "dist"),
        check_vma=False,
    )
```

time: 357 us -> 55.3 us (0.15)
  waiting for transfers between devices: 158 us -> 0 us
  blocking collectives: 98 us -> 0 us
  Pallas kernels: 0 us -> 45.7 us
  starting transfers between devices: 31.3 us -> 0 us
  local copies, waits for them, and re-layouts: 30.2 us -> 5.31 us
  matrix products: 18.1 us -> 0 us
  between operations: 14.2 us -> 0.12 us
    all_to_all x1 -> x0, waiting for transfers between devices: 105 us -> none  [local(): lax.all_to_all(whole_rows, 'dist', split_axis=1, concat_axis=0, tiled=True)]
    unnamed x1 -> x0, blocking collectives: 98 us -> none
    all_gather x1 -> x0, waiting for transfers between devices: 50.9 us -> none  [local(): whole_rows = lax.all_gather(int_masked, 'rep', axis=1, tiled=True)]
    pallas_call x0 -> x1, Pallas kernels: none -> 45.7 us  [local(): pl.pallas_call(kernel, out_shape=jax.ShapeDtypeStruct((BJ, MY), F32), in_...]
    unnamed x6 -> x0, starting transfers between devices: 20.4 us -> none
    all_to_all x3 -> x0, local copies, waits for them, and re-layouts: 19 us -> none  [local(): lax.all_to_all(whole_rows, 'dist', split_axis=1, concat_axis=0, tiled=True)]
    dot_general x1 -> x0, matrix products: 18.1 us -> none  [local(): lax.dot_general(amp_masked, int_blocks, (((1,), (1,)), ((), ())), precisi...]
    all_to_all x1 -> x0, starting transfers between devices: 10.9 us -> none  [local(): lax.all_to_all(whole_rows, 'dist', split_axis=1, concat_axis=0, tiled=True)]
  transfers between devices with their start and end apart: 8 -> 0, of which waited for: 3 -> 0; matrix products, arithmetic and copies ran while one was open for 0% -> 0% of each run, Pallas kernels for 0% -> 0%
where the time goes in v1:
time: 55.3 us; the launch traced here: 55.1 us
  Pallas kernels  45.7 us (83%)
  local copies, waits for them, and re-layouts  5.31 us (10%)
  other arithmetic  3.9 us (7%)
    pallas_call x1, Pallas kernels, local(): pl.pallas_call(kernel, out_shape=jax.ShapeDtypeStruct((BJ, MY), F32), in_...  45.7 us
    unnamed x5, local copies, waits for them, and re-layouts  3.81 us

profile of v1, /device:TPU:1, one launch (start us, length us, event | category | flops | bytes accessed | tf_op | source)
XLA Modules:
  0.0 55.1 jit_solution(16269578732732224114)
XLA Ops:
  0.0 0.9 %broadcast_xor_fusion = s32[1200,16]{1,0:T(8,128)S(1)} fusion(s32[16]{0:T(128)} %param.11, s32[1200]{0:T(1024)} %param.10), kind=kLoop, calls=%fused_computation | loop fusion | flops 19200 | bytes 81664 | tf_op jit(solution)/shard_map/xor | solution.py:317
  0.9 0.2 xor.51
  1.2 0.9 %convert_reduce_fusion.1 = s32[16]{0:T(128)S(1)} fusion(s32[16]{0:T(128)} %param.11), kind=kLoop, calls=%fused_computation.12 | loop fusion | flops 1264 | bytes 128 | tf_op jit(solution)/shard_map/reduce_sum | solution.py:321
  2.1 0.1 tile.9
  2.2 0.1 fusion.8
  2.2 0.1 broadcast_in_dim.51.a_col_sym
  2.4 0.8 %broadcast_xor_fusion.1 = s32[176,16]{1,0:T(8,128)S(1)} fusion(s32[16]{0:T(128)} %param.11, s32[176]{0:T(256)} %param.9), kind=kLoop, calls=%fused_computation.2 | loop fusion | flops 2816 | bytes 12032 | tf_op jit(solution)/shard_map/xor | solution.py:316
  3.2 0.1 xor.52
  3.3 0.1 dynamic_slice.23
  3.4 0.2 convert_reduce_fusion
  3.6 0.1 multiply_add_fusion
  3.7 0.1 copy.17.bj_code_col
  3.8 0.1 copy.16.bj_sym
  3.9 0.8 %broadcast_subtract_fusion = f32[176,16]{1,0:T(8,128)S(1)} fusion(f32[176]{0:T(256)} %param.13, f32[16]{0:T(128)} %param.12), kind=kLoop, calls=%fused_computation.1 | loop fusion | flops 2816 | bytes 12032 | tf_op jit(solution)/shard_map/sub | solution.py:318
  4.7 0.1 sub.47
  4.8 0.1 dynamic_slice.27
  4.9 0.1 copy.18.bj_shift
  5.2 0.1 dynamic_slice.22
  5.3 0.1 xor.47.row_sym
  5.4 0.1 tile.21
  5.5 2.0 %copy-done = f32[2816,300]{0,1:T(8,128)S(1)} copy-done((f32[2816,300]{0,1:T(8,128)S(1)}, f32[2816,300]{0,1:T(8,128)}, u32[]{:S(2)}) %copy-start) | copy-done | bytes 3379224
  7.5 1.2 %copy-done.1 = f32[44,4800]{1,0:T(8,128)S(1)} copy-done((f32[44,4800]{1,0:T(8,128)S(1)}, f32[44,4800]{1,0:T(8,128)}, u32[]{:S(2)}) %copy-start.1) | copy-done | bytes 844824
  8.7 45.7 %shard_map.73 = f32[44,704]{1,0:T(8,128)S(1)} custom-call(f32[300,2816]{1,0:T(8,128)S(1)} %bitcast.10, f32[44,4800]{1,0:T(8,128)S(1)} %copy-done.1, s32[1,2816]{1,0:T(1,128)S(1)} %xor.47.row_sym, s32[300,1]{1,0:T(8,128)S(1)} %broadcast_in_dim.51.a_col_sym, s32[1,4800]{1,0:T(1,128)S(1)} %broadcast_in_dim.19.w_col_sym, s32[48,1]{1,0:T(8,128)S(1)} %copy.16.bj_sym, ...), custom_call_target="tpu_custom_call" | custom-call | tf_op jit(solution)/shard_map/pallas_call | solution.py:346
  54.4 0.7 %copy.20 = f32[704,44]{0,1:T(8,128)} copy(f32[704,44]{0,1:T(8,128)S(1)} %bitcast.11) | data formatting | bytes 247808
  (17 shorter events, 0.4 us)
Async XLA Ops:
  5.5 2.0 %copy-start = (f32[2816,300]{0,1:T(8,128)S(1)}, f32[2816,300]{0,1:T(8,128)}, u32[]{:S(2)}) copy-start(f32[2816,300]{0,1:T(8,128)} %param.7) | copy-start | bytes 10137604
  7.5 1.2 %copy-start.1 = (f32[44,4800]{1,0:T(8,128)S(1)}, f32[44,4800]{1,0:T(8,128)}, u32[]{:S(2)}) copy-start(f32[44,4800]{1,0:T(8,128)} %w_hbm.1) | copy-start | bytes 2534404

commit v2 on v1

--- a/solution.py
+++ b/solution.py
@@ -59,6 +59,7 @@
     pick,
     a_msg,
     w_msg,
+    w_mid,
     a_got,
     w_got,
     a_all,
@@ -66,9 +67,11 @@
     o_got,
     load_sem,
     a_send,
+    x_send,
     w_send,
     o_send,
     a_recv,
+    x_recv,
     w_recv,
     o_recv,
 ):
@@ -76,10 +79,6 @@
     x = lax.axis_index("rep")
     z, place = d // PLACES, d % PLACES
     y, core = place // 2, place % 2
-    home_y = (x - y + Y) % Y
-    self_w = jnp.where((z // 2 == x) & (home_y == y), 1, 0)
-    self_o = jnp.where(home_y == y, 1, 0)
-
     load_a = pltpu.make_async_copy(a_hbm, a_in, load_sem.at[0])
     load_w = pltpu.make_async_copy(w_hbm, w_in, load_sem.at[1])
     load_w.start()
@@ -94,31 +93,13 @@
         greet(z * PLACES + (place + i) % PLACES, x)
         return carry
 
-    def greet_w(i, carry):
-        zs = (z + i // 2) % Z
-        cs = i % 2
-        dd, xx = zs * PLACES + home_y * 2 + cs, z // 2
-
-        @pl.when(jnp.logical_not((dd == d) & (xx == x)))
-        def _():
-            greet(dd, xx)
-
-        return carry
-
     def greet_o(i, carry):
-        zs = (z + i // PLACES) % Z
-        s = (place + i) % PLACES
-        dd, xx = zs * PLACES + s, (y + s // 2) % Y
-
-        @pl.when(jnp.logical_not((dd == d) & (xx == x)))
-        def _():
-            greet(dd, xx)
-
-        return carry
-
-    lax.fori_loop(1, PLACES, greet_a, 0)
-    lax.fori_loop(0, 2 * Z, greet_w, 0)
-    lax.fori_loop(0, Z * PLACES, greet_o, 0)
+        zs, cs, xs = (z + i // PLACES) % Z, (core + i) % 2, (x + (i % PLACES) // 2) % X
+        greet(zs * PLACES + y * 2 + cs, xs)
+        return carry
+
+    lax.fori_loop(2 - core, PLACES - core, greet_a, 0)
+    lax.fori_loop(1, Z * PLACES, greet_o, 0)
 
     for n in range(8):
         cols = pl.ds(n * 256, 256)
@@ -147,44 +128,29 @@
         rows = slice(half * 2 * BPAD, (half + 1) * 2 * BPAD)
         main = matmul(group, w_main[rows].astype(BF16), NN)
         rest = matmul(group, w_rest[rows].astype(BF16), NN)
-        w_msg[half, :, :, pl.ds(0, 256)] = main.reshape(IRREPS, 8, 256)
-        w_msg[half, :, :, pl.ds(256, 128)] = rest.reshape(IRREPS, 8, 128)
-
-    pl.semaphore_wait(barrier, 7 + 2 * Z - self_w + Z * PLACES - self_o)
-
-    slot_w = z * 2 + core
-
-    def w_route(i):
-        half = i // PLACES
-        s = (place + i) % PLACES
-        dd, xx = (2 * x + half) * PLACES + s, (y + s // 2) % Y
-        return half, s, dd, xx, (dd == d) & (xx == x)
-
-    def w_copy(i):
-        half, s, dd, xx, _ = w_route(i)
+        w_msg[:, half, :, pl.ds(0, 256)] = main.reshape(IRREPS, 8, 256)
+        w_msg[:, half, :, pl.ds(256, 128)] = rest.reshape(IRREPS, 8, 128)
+
+    pl.semaphore_wait(barrier, 6 + Z * PLACES - 1)
+
+    def x_copy(i):
+        cs, xs = (core + i // 3) % 2, (x + 1 + i % 3) % X
         return pltpu.make_async_remote_copy(
-            src_ref=w_msg.at[half, s],
-            dst_ref=w_got.at[slot_w],
-            send_sem=w_send.at[i],
-            recv_sem=w_recv,
-            device_id=(dd, xx),
+            src_ref=w_msg.at[2 * xs + cs],
+            dst_ref=w_mid.at[cs, x],
+            send_sem=x_send.at[i],
+            recv_sem=x_recv.at[cs],
+            device_id=(d, xs),
             device_id_type=MESH,
         )
 
-    def send_w(i, carry):
-        half, s, dd, xx, mine = w_route(i)
-
-        @pl.when(mine)
-        def _():
-            pltpu.make_async_copy(w_msg.at[half, s], w_got.at[slot_w], w_recv).start()
-
-        @pl.when(jnp.logical_not(mine))
-        def _():
-            w_copy(i).start()
-
-        return carry
-
-    lax.fori_loop(0, 2 * PLACES, send_w, 0)
+    def send_x(i, carry):
+        x_copy(i).start()
+        return carry
+
+    lax.fori_loop(0, 6, send_x, 0)
+    for cs in range(2):
+        pltpu.make_async_copy(w_msg.at[2 * x + cs], w_mid.at[cs, x], x_recv.at[cs]).start()
 
     load_a.wait()
     for n in range(11):
@@ -197,21 +163,23 @@
     a_rest = matmul(
         a_split[:, pl.ds(2048, ROWS - 2048)], pick[pl.ds(0, 128), pl.ds(0, ROWS - 2048)], NT
     )
-    place_rows = lax.broadcasted_iota(I32, (IRREPS * SLOTS, 2 * APAD), 0) == a_code[...]
+    place_rows = lax.broadcasted_iota(I32, (2 * SLOTS, 2 * APAD), 0) == (
+        a_code[...] - 2 * SLOTS * x
+    )
     place_rows = place_rows.astype(F32).astype(BF16)
     main = matmul(place_rows, a_main.astype(BF16), NN)
     rest = matmul(place_rows, a_rest.astype(BF16), NN)
-    a_msg[:, :, pl.ds(0, 256)] = main.reshape(IRREPS, SLOTS, 256)
-    a_msg[:, :, pl.ds(256, 128)] = rest.reshape(IRREPS, SLOTS, 128)
+    a_msg[:, :, pl.ds(0, 256)] = main.reshape(2, SLOTS, 256)
+    a_msg[:, :, pl.ds(256, 128)] = rest.reshape(2, SLOTS, 128)
 
     def a_copy(i):
-        s = (place + i) % PLACES
+        to = (place + i) % PLACES
         return pltpu.make_async_remote_copy(
-            src_ref=a_msg.at[s],
+            src_ref=a_msg.at[to % 2],
             dst_ref=a_got.at[place],
             send_sem=a_send.at[i],
             recv_sem=a_recv,
-            device_id=(z * PLACES + s, x),
+            device_id=(z * PLACES + to, x),
             device_id_type=MESH,
         )
 
@@ -220,7 +188,31 @@
         return carry
 
     lax.fori_loop(1, PLACES, send_a, 0)
-    pltpu.make_async_copy(a_msg.at[place], a_got.at[place], a_recv).start()
+    pltpu.make_async_copy(a_msg.at[core], a_got.at[place], a_recv).start()
+
+    slot_w = z * 2 + core
+
+    def w_copy(i):
+        cs, zs = (core + i // Z) % 2, (z + i) % Z
+        return pltpu.make_async_remote_copy(
+            src_ref=w_mid.at[cs, zs // 2, zs % 2],
+            dst_ref=w_got.at[slot_w],
+            send_sem=w_send.at[i],
+            recv_sem=w_recv,
+            device_id=(zs * PLACES + y * 2 + cs, x),
+            device_id_type=MESH,
+        )
+
+    def send_w(i, carry):
+        w_copy(i).start()
+        return carry
+
+    first, second = w_mid.at[core], w_mid.at[1 - core]
+    pltpu.make_async_copy(first, first, x_recv.at[core]).wait()
+    pltpu.make_async_copy(first.at[z // 2, z % 2], w_got.at[slot_w], w_recv).start()
+    lax.fori_loop(1, Z, send_w, 0)
+    pltpu.make_async_copy(second, second, x_recv.at[1 - core]).wait()
+    lax.fori_loop(Z, 2 * Z, send_w, 0)
 
     a_all[...] = jnp.zeros(a_all.shape, F32)
     pltpu.make_async_copy(a_got, a_got, a_recv).wait()
@@ -237,38 +229,25 @@
             2 * Z, 8, QA
         )
 
-    def o_route(i):
-        zs = (z + i // PLACES) % Z
-        cs = (core + i) % 2
-        part = (x + (i % PLACES) // 2) % X
-        dd = zs * PLACES + home_y * 2 + cs
-        return zs * 2 + cs, part, dd, (dd == d) & (part == x)
-
     def o_copy(i):
-        w, part, dd, _ = o_route(i)
+        zs, cs, part = (z + i // PLACES) % Z, (core + i) % 2, (x + (i % PLACES) // 2) % X
         return pltpu.make_async_remote_copy(
-            src_ref=o_msg.at[part, w],
-            dst_ref=o_got.at[d],
+            src_ref=o_msg.at[part, zs * 2 + cs],
+            dst_ref=o_got.at[z * PLACES + 2 * x + core],
             send_sem=o_send.at[i],
             recv_sem=o_recv,
-            device_id=(dd, part),
+            device_id=(zs * PLACES + y * 2 + cs, part),
             device_id_type=MESH,
         )
 
     def send_o(i, carry):
-        w, part, dd, mine = o_route(i)
-
-        @pl.when(mine)
-        def _():
-            pltpu.make_async_copy(o_msg.at[part, w], o_got.at[d], o_recv).start()
-
-        @pl.when(jnp.logical_not(mine))
-        def _():
-            o_copy(i).start()
-
-        return carry
-
-    lax.fori_loop(0, Z * PLACES, send_o, 0)
+        o_copy(i).start()
+        return carry
+
+    lax.fori_loop(1, Z * PLACES, send_o, 0)
+    pltpu.make_async_copy(
+        o_msg.at[x, slot_w], o_got.at[z * PLACES + 2 * x + core], o_recv
+    ).start()
 
     spread = (
         lax.broadcasted_iota(I32, (BPAD, 128), 1) % 64 == bj_code_col[...]
@@ -285,11 +264,12 @@
     value = jnp.where(bj_sym[...] == out_sym[...], cycle, 0.0) / (out_shift[...] + bj_shift[...])
     out_ref[...] = value[:BJ]
 
+    def done_x(i, carry):
+        x_copy(i).wait_send()
+        return carry
+
     def done_w(i, carry):
-        @pl.when(jnp.logical_not(w_route(i)[4]))
-        def _():
-            w_copy(i).wait_send()
-
+        w_copy(i).wait_send()
         return carry
 
     def done_a(i, carry):
@@ -297,15 +277,13 @@
         return carry
 
     def done_o(i, carry):
-        @pl.when(jnp.logical_not(o_route(i)[3]))
-        def _():
-            o_copy(i).wait_send()
-
-        return carry
-
-    lax.fori_loop(0, 2 * PLACES, done_w, 0)
+        o_copy(i).wait_send()
+        return carry
+
+    lax.fori_loop(0, 6, done_x, 0)
+    lax.fori_loop(1, 2 * Z, done_w, 0)
     lax.fori_loop(1, PLACES, done_a, 0)
-    lax.fori_loop(0, Z * PLACES, done_o, 0)
+    lax.fori_loop(1, Z * PLACES, done_o, 0)
 
 
 def local(
@@ -354,8 +332,9 @@
             pltpu.VMEM((2 * APAD, ROWS), BF16),
             pltpu.VMEM((4 * BPAD, 2432), BF16),
             pltpu.VMEM((256, 2048), BF16),
-            pltpu.VMEM((IRREPS, SLOTS, 384), F32),
-            pltpu.VMEM((2, IRREPS, 8, 384), F32),
+            pltpu.VMEM((2, SLOTS, 384), F32),
+            pltpu.VMEM((IRREPS, 2, 8, 384), F32),
+            pltpu.VMEM((2, X, 2, 8, 384), F32),
             pltpu.VMEM((PLACES, SLOTS, 384), F32),
             pltpu.VMEM((2 * Z, 8, 384), F32),
             pltpu.VMEM((384, 384), F32),
@@ -363,14 +342,16 @@
             pltpu.VMEM((Z * PLACES, 8, 128), F32),
             pltpu.SemaphoreType.DMA((2,)),
             pltpu.SemaphoreType.DMA((PLACES,)),
-            pltpu.SemaphoreType.DMA((2 * PLACES,)),
+            pltpu.SemaphoreType.DMA((6,)),
+            pltpu.SemaphoreType.DMA((2 * Z,)),
             pltpu.SemaphoreType.DMA((Z * PLACES,)),
             pltpu.SemaphoreType.DMA,
+            pltpu.SemaphoreType.DMA((2,)),
             pltpu.SemaphoreType.DMA,
             pltpu.SemaphoreType.DMA,
         ],
         compiler_params=pltpu.CompilerParams(
-            collective_id=0, has_side_effects=True, vmem_limit_bytes=48 * 1024 * 1024
+            collective_id=0, has_side_effects=True, vmem_limit_bytes=52 * 1024 * 1024
         ),
     )(
         amplitudes.T,

time: 55.3 us -> 42.6 us (0.77)
  Pallas kernels: 45.7 us -> 35.1 us
  local copies, waits for them, and re-layouts: 5.31 us -> 3.34 us
    pallas_call x1, Pallas kernels: 45.7 us -> 35.1 us  [local(): pl.pallas_call(kernel, out_shape=jax.ShapeDtypeStruct((BJ, MY), F32), in_...]
    unnamed x5 -> x3, local copies, waits for them, and re-layouts: 3.81 us -> 1.84 us
where the time goes in v2:
time: 42.6 us; the launch traced here: 42.4 us
  Pallas kernels  35.1 us (82%)
  other arithmetic  3.9 us (9%)
  local copies, waits for them, and re-layouts  3.34 us (8%)
    pallas_call x1, Pallas kernels, local(): pl.pallas_call(kernel, out_shape=jax.ShapeDtypeStruct((BJ, MY), F32), in_...  35.1 us
    unnamed x3, local copies, waits for them, and re-layouts  1.84 us
    xor x1, other arithmetic, local(): col_sym = (virtual_irrep[:, None] ^ occupied_irrep[None, :]).reshape(-1)  0.93 us
    reduce_sum x1, other arithmetic, local(): rank = jnp.sum((same & earlier).astype(I32), axis=1)  0.91 us

profile of v2, /device:TPU:1, one launch (start us, length us, event | category | flops | bytes accessed | tf_op | source)
XLA Modules:
  0.0 42.4 jit_solution(466098271388660617)
XLA Ops:
  0.0 0.9 %broadcast_xor_fusion = s32[1200,16]{1,0:T(8,128)S(1)} fusion(s32[16]{0:T(128)} %param.11, s32[1200]{0:T(1024)} %param.10), kind=kLoop, calls=%fused_computation | loop fusion | flops 19200 | bytes 81664 | tf_op jit(solution)/shard_map/xor | solution.py:295
  0.9 0.2 xor.51
  1.2 0.9 %convert_reduce_fusion.1 = s32[16]{0:T(128)S(1)} fusion(s32[16]{0:T(128)} %param.11), kind=kLoop, calls=%fused_computation.12 | loop fusion | flops 1264 | bytes 128 | tf_op jit(solution)/shard_map/reduce_sum | solution.py:299
  2.1 0.1 tile.9
  2.2 0.1 fusion.8
  2.2 0.1 broadcast_in_dim.51.a_col_sym
  2.4 0.1 pad_add_fusion
  2.4 0.8 %broadcast_xor_fusion.1 = s32[176,16]{1,0:T(8,128)S(1)} fusion(s32[16]{0:T(128)} %param.11, s32[176]{0:T(256)} %param.9), kind=kLoop, calls=%fused_computation.2 | loop fusion | flops 2816 | bytes 12032 | tf_op jit(solution)/shard_map/xor | solution.py:294
  3.2 0.1 xor.52
  3.3 0.1 dynamic_slice.23
  3.4 0.2 convert_reduce_fusion
  3.6 0.1 multiply_add_fusion
  3.7 0.1 copy.17.bj_code_col
  3.8 0.1 copy.16.bj_sym
  3.9 0.8 %broadcast_subtract_fusion = f32[176,16]{1,0:T(8,128)S(1)} fusion(f32[176]{0:T(256)} %param.13, f32[16]{0:T(128)} %param.12), kind=kLoop, calls=%fused_computation.1 | loop fusion | flops 2816 | bytes 12032 | tf_op jit(solution)/shard_map/sub | solution.py:296
  4.7 0.1 sub.47
  4.8 0.1 dynamic_slice.27
  4.9 0.1 copy.18.bj_shift
  5.2 0.1 dynamic_slice.22
  5.3 0.1 xor.47.row_sym
  5.4 0.1 tile.21
  5.5 1.2 %copy-done = f32[44,4800]{1,0:T(8,128)S(1)} copy-done((f32[44,4800]{1,0:T(8,128)S(1)}, f32[44,4800]{1,0:T(8,128)}, u32[]{:S(2)}) %copy-start) | copy-done | bytes 844824
  6.7 35.1 %shard_map.73 = f32[44,704]{1,0:T(8,128)S(1)} custom-call(f32[300,2816]{1,0:T(8,128)} %bitcast.11, f32[44,4800]{1,0:T(8,128)S(1)} %copy-done, s32[1,2816]{1,0:T(1,128)S(1)} %xor.47.row_sym, s32[300,1]{1,0:T(8,128)S(1)} %broadcast_in_dim.51.a_col_sym, s32[1,4800]{1,0:T(1,128)S(1)} %broadcast_in_dim.19.w_col_sym, s32[48,1]{1,0:T(8,128)S(1)} %copy.16.bj_sym, ...), custom_call_target="tpu_custom_call" | custom-call | tf_op jit(solution)/shard_map/pallas_call | solution.py:324
  41.8 0.7 %copy.20 = f32[704,44]{0,1:T(8,128)} copy(f32[704,44]{0,1:T(8,128)S(1)} %bitcast.10) | data formatting | bytes 247808
  (15 shorter events, 0.3 us)
Async XLA Ops:
  5.5 1.2 %copy-start = (f32[44,4800]{1,0:T(8,128)S(1)}, f32[44,4800]{1,0:T(8,128)}, u32[]{:S(2)}) copy-start(f32[44,4800]{1,0:T(8,128)} %w_hbm.1) | copy-start | bytes 2534404

commit v3 on v2

--- a/solution.py
+++ b/solution.py
@@ -37,20 +37,44 @@
 NT = ((1,), (1,))
 
 
+def iota(shape, dim):
+    return lax.broadcasted_iota(I32, shape, dim)
+
+
+def exact(left, right, dims):
+    return lax.dot_general(
+        left, right, (dims, ((), ())), precision=lax.Precision.HIGHEST, preferred_element_type=F32
+    )
+
+
+def one_hot(mask):
+    return mask.astype(F32)
+
+
+def small(mask):
+    return mask.astype(F32).astype(BF16)
+
+
+def tiles(values, offset, count):
+    size = values.shape[1]
+    at = iota((count, size), 1) - offset
+    parts = jnp.where((at >> 3) == iota((count, size), 0), values, 0.0)
+    spread = ((iota((size, 128), 0) - offset) & 7) == (iota((size, 128), 1) >> 4)
+    return parts, spread
+
+
+def side_by_side(rows, first, count):
+    return jnp.concatenate([rows[first + n : first + n + 1] for n in range(count)], axis=1)
+
+
 def kernel(
     a_hbm,
     w_hbm,
-    row_sym,
-    a_col_sym,
-    w_col_sym,
-    bj_sym,
-    a_code,
-    bj_code,
-    bj_code_col,
-    rank_key,
-    out_sym,
-    out_shift,
-    bj_shift,
+    slab_ref,
+    virtual_ref,
+    occupied_ref,
+    occupied_energy_ref,
+    slab_energy_ref,
     out_ref,
     a_in,
     w_in,
@@ -63,6 +87,7 @@
     a_got,
     w_got,
     a_all,
+    w_sym,
     o_msg,
     o_got,
     load_sem,
@@ -101,10 +126,84 @@
     lax.fori_loop(2 - core, PLACES - core, greet_a, 0)
     lax.fori_loop(1, Z * PLACES, greet_o, 0)
 
-    for n in range(8):
-        cols = pl.ds(n * 256, 256)
-        slot = lax.broadcasted_iota(I32, (256, 256), 0)
-        pick[:, cols] = (rank_key[:, cols] == slot).astype(F32).astype(BF16)
+    slab = slab_ref[...].reshape(1, -1).astype(F32)
+    virtual = virtual_ref[...].reshape(1, -1).astype(F32)
+    occupied = occupied_ref[...].reshape(1, -1).astype(F32)
+    occupied_energy = occupied_energy_ref[...].reshape(1, -1)
+    slab_energy = slab_energy_ref[...].reshape(1, -1)
+    n_slab, n_virtual = slab.shape[1], virtual.shape[1]
+    slab_all = jnp.broadcast_to(slab, (128, n_slab)).astype(BF16)
+    occ_all = jnp.broadcast_to(occupied, (128, O)).astype(BF16)
+
+    repeat = iota((O, 128), 0) == (iota((O, 128), 1) & 15)
+    occ_lane = matmul(occ_all[:16], small(repeat), NN)[:1].astype(I32)
+    occ_energy_lane = exact(jnp.broadcast_to(occupied_energy, (8, O)), one_hot(repeat), NN)[:1]
+    occ_col = matmul(small(iota((O, O), 0) == iota((O, O), 1)), occ_all, NT).astype(I32)
+    earlier = (occ_col == occ_lane) & (iota((O, 128), 0) < (iota((O, 128), 1) & 15))
+    rank = jnp.sum(one_hot(earlier), axis=0, keepdims=True)
+    key = 2 * (iota((1, 128), 1) >> 4) + rank.astype(I32)
+
+    parts, spread = tiles(slab, 0, 32)
+    row_sym = matmul(parts.astype(BF16), small(spread), NN).astype(I32) ^ occ_lane
+    parts, spread = tiles(slab, (MY // O) * x, 16)
+    out_sym = matmul(parts.astype(BF16), small(spread), NN).astype(I32) ^ occ_lane
+    parts, _ = tiles(slab_energy, (MY // O) * x, 8)
+    out_shift = occ_energy_lane - exact(parts, one_hot(spread), NN)
+    out_sym = side_by_side(out_sym, 0, 6)[:, :MY]
+    out_shift = side_by_side(out_shift, 0, 6)[:, :MY]
+
+    parts, spread = tiles(virtual, (WIDE // O) * x, 48)
+    columns = matmul(parts.astype(BF16), small(spread), NN).astype(I32) ^ occ_lane
+    for n in range(38):
+        w_sym[:, pl.ds(n * 128, 128)] = columns[n : n + 1]
+
+    first_c, inside = (COLS * d) // O, (COLS * d) % O
+    near = small(iota((n_virtual, 128), 0) == first_c + iota((n_virtual, 128), 1))
+    near = matmul(jnp.broadcast_to(virtual, (16, n_virtual)).astype(BF16), near, NN)
+    near_all = jnp.broadcast_to(near[:1], (128, 128)).astype(BF16)
+    at = inside + iota((APAD, 128), 0)
+    v_col = matmul(small((at >> 4) == iota((APAD, 128), 1)), near_all, NT).astype(I32)
+    at = inside + iota((APAD, O), 0)
+    o_col = matmul(small((at & 15) == iota((APAD, O), 1)), occ_all, NT).astype(I32)
+    a_col_sym = (v_col ^ o_col)[:COLS, :1]
+    at = inside + iota((128, 384), 1)
+    v_row = matmul(near_all[:16], small((at >> 4) == iota((128, 384), 0)), NN)[:1].astype(I32)
+    at = inside + iota((O, 384), 1)
+    pick_o = small((at & 15) == iota((O, 384), 0))
+    o_row = matmul(occ_all[:16], pick_o, NN)[:1].astype(I32)
+    rank_all = jnp.broadcast_to(rank[:, :O], (16, O)).astype(BF16)
+    rank_row = matmul(rank_all, pick_o, NN)[:1].astype(I32)
+    at = inside + iota((1, 384), 1)
+    a_code = SLOTS * ((v_row ^ o_row) - 2 * x) + 2 * (at >> 4) + rank_row
+    a_code = jnp.where(iota((1, 384), 1) < COLS, a_code, -1)[:, :APAD]
+
+    at = BJ * d + iota((BPAD, n_slab), 0)
+    pick_b = (at >> 4) == iota((BPAD, n_slab), 1)
+    at = BJ * d + iota((BPAD, O), 0)
+    pick_j = (at & 15) == iota((BPAD, O), 1)
+    bj_col = matmul(small(pick_b), slab_all, NT).astype(I32) ^ matmul(
+        small(pick_j), occ_all, NT
+    ).astype(I32)
+    bj_sym = jnp.where(iota((BPAD, 128), 0) < BJ, bj_col, -1)
+    bj_shift = (
+        exact(one_hot(pick_j), jnp.broadcast_to(occupied_energy, (128, O)), NT)
+        - exact(one_hot(pick_b), jnp.broadcast_to(slab_energy, (128, n_slab)), NT)
+    )[:, :1]
+    at = BJ * d + iota((n_slab, 128), 1)
+    b_row = matmul(slab_all[:16], small((at >> 4) == iota((n_slab, 128), 0)), NN)[:1]
+    at = BJ * d + iota((O, 128), 1)
+    j_row = matmul(occ_all[:16], small((at & 15) == iota((O, 128), 0)), NN)[:1]
+    bj_row = jnp.where(iota((1, 128), 1) < BJ, b_row.astype(I32) ^ j_row.astype(I32), -1)
+    same = bj_sym == bj_row
+    shape = (BPAD, 128)
+    slot_row = jnp.sum(one_hot(same & (iota(shape, 0) < iota(shape, 1))), axis=0, keepdims=True)
+    slot_col = jnp.sum(one_hot(same & (iota(shape, 1) < iota(shape, 0))), axis=1, keepdims=True)
+    bj_code = jnp.where(bj_row < 0, -1, 8 * bj_row + slot_row.astype(I32))[:, :BPAD]
+    bj_sym = bj_sym[:, :1]
+    bj_code_col = jnp.where(bj_sym < 0, -1, 8 * bj_sym + slot_col.astype(I32))
+
+    for n in range(16):
+        pick[:, pl.ds(n * 128, 128)] = small(key + 16 * n == iota((256, 128), 0))
     for n in range(4):
         o_msg[n] = jnp.zeros((2 * Z, 8, 128), F32)
         w_split[pl.ds(n * BPAD + 32, 16)] = jnp.zeros((16, 2432), BF16)
@@ -114,7 +213,7 @@
     load_w.wait()
     for half in range(2):
         cols = pl.ds(half * HALF, HALF)
-        kept = jnp.where(bj_sym[pl.ds(0, BJ)] == w_col_sym[:, cols], w_in[:, cols], 0.0)
+        kept = jnp.where(bj_sym[:BJ] == w_sym[:, cols], w_in[:, cols], 0.0)
         high, low = halves(kept)
         w_split[pl.ds(half * 2 * BPAD, BJ), pl.ds(0, HALF)] = high
         w_split[pl.ds((half * 2 + 1) * BPAD, BJ), pl.ds(0, HALF)] = low
@@ -122,12 +221,11 @@
     w_rest = matmul(
         w_split[:, pl.ds(2048, HALF - 2048)], pick[pl.ds(0, 128), pl.ds(0, HALF - 2048)], NT
     )
-    group = lax.broadcasted_iota(I32, (IRREPS * 8, 2 * BPAD), 0) == bj_code[...]
-    group = group.astype(F32).astype(BF16)
+    group = small(iota((IRREPS * 8, BPAD), 0) == bj_code)
     for half in range(2):
-        rows = slice(half * 2 * BPAD, (half + 1) * 2 * BPAD)
-        main = matmul(group, w_main[rows].astype(BF16), NN)
-        rest = matmul(group, w_rest[rows].astype(BF16), NN)
+        rows = [slice((2 * half + n) * BPAD, (2 * half + n + 1) * BPAD) for n in range(2)]
+        main = sum(matmul(group, w_main[r].astype(BF16), NN) for r in rows)
+        rest = sum(matmul(group, w_rest[r].astype(BF16), NN) for r in rows)
         w_msg[:, half, :, pl.ds(0, 256)] = main.reshape(IRREPS, 8, 256)
         w_msg[:, half, :, pl.ds(256, 128)] = rest.reshape(IRREPS, 8, 128)
 
@@ -155,7 +253,9 @@
     load_a.wait()
     for n in range(11):
         cols = pl.ds(n * 256, 256)
-        kept = jnp.where(a_col_sym[...] == row_sym[:, cols], a_in[:, cols], 0.0)
+        kept = jnp.where(
+            a_col_sym == side_by_side(row_sym, 2 * n, 2), a_in[:, cols], 0.0
+        )
         high, low = halves(kept)
         a_split[pl.ds(0, COLS), cols] = high
         a_split[pl.ds(APAD, COLS), cols] = low
@@ -163,12 +263,10 @@
     a_rest = matmul(
         a_split[:, pl.ds(2048, ROWS - 2048)], pick[pl.ds(0, 128), pl.ds(0, ROWS - 2048)], NT
     )
-    place_rows = lax.broadcasted_iota(I32, (2 * SLOTS, 2 * APAD), 0) == (
-        a_code[...] - 2 * SLOTS * x
-    )
-    place_rows = place_rows.astype(F32).astype(BF16)
-    main = matmul(place_rows, a_main.astype(BF16), NN)
-    rest = matmul(place_rows, a_rest.astype(BF16), NN)
+    place_rows = small(iota((2 * SLOTS, APAD), 0) == a_code)
+    rows = [slice(n * APAD, (n + 1) * APAD) for n in range(2)]
+    main = sum(matmul(place_rows, a_main[r].astype(BF16), NN) for r in rows)
+    rest = sum(matmul(place_rows, a_rest[r].astype(BF16), NN) for r in rows)
     a_msg[:, :, pl.ds(0, 256)] = main.reshape(2, SLOTS, 256)
     a_msg[:, :, pl.ds(256, 128)] = rest.reshape(2, SLOTS, 128)
 
@@ -249,9 +347,7 @@
         o_msg.at[x, slot_w], o_got.at[z * PLACES + 2 * x + core], o_recv
     ).start()
 
-    spread = (
-        lax.broadcasted_iota(I32, (BPAD, 128), 1) % 64 == bj_code_col[...]
-    ).astype(F32).astype(BF16)
+    spread = small((iota((BPAD, 128), 1) & 63) == bj_code_col)
     pltpu.make_async_copy(o_got, o_got, o_recv).wait()
     total = o_got[pl.ds(0, PLACES)]
     for zs in range(1, Z):
@@ -261,7 +357,7 @@
     high, low = halves(mine)
     widen = pick[pl.ds(0, 128), pl.ds(0, MY)]
     cycle = matmul(high, widen, NN) + matmul(low, widen, NN)
-    value = jnp.where(bj_sym[...] == out_sym[...], cycle, 0.0) / (out_shift[...] + bj_shift[...])
+    value = jnp.where(bj_sym == out_sym, cycle, 0.0) / (out_shift + bj_shift)
     out_ref[...] = value[:BJ]
 
     def done_x(i, carry):
@@ -289,42 +385,12 @@
 def local(
     amplitudes, integrals, slab_irrep, virtual_irrep, occupied_irrep, occupied_energy, slab_energy
 ):
-    d = lax.axis_index("dist")
-    x = lax.axis_index("rep")
-    row_sym = (slab_irrep[:, None] ^ occupied_irrep[None, :]).reshape(-1)
-    col_sym = (virtual_irrep[:, None] ^ occupied_irrep[None, :]).reshape(-1)
-    shifts = (occupied_energy[None, :] - slab_energy[:, None]).reshape(-1)
-    same = occupied_irrep[:, None] == occupied_irrep[None, :]
-    earlier = jnp.arange(O)[None, :] < jnp.arange(O)[:, None]
-    rank = jnp.sum((same & earlier).astype(I32), axis=1)
-
-    a_sym = lax.dynamic_slice_in_dim(col_sym, d * COLS, COLS, 0)
-    w_sym = lax.dynamic_slice_in_dim(col_sym, x * WIDE, WIDE, 0)
-    bj_sym = lax.dynamic_slice_in_dim(row_sym, d * BJ, BJ, 0)
-    out_sym = lax.dynamic_slice_in_dim(row_sym, x * MY, MY, 0)
-    bj_shift = lax.dynamic_slice_in_dim(shifts, d * BJ, BJ, 0)
-    out_shift = lax.dynamic_slice_in_dim(shifts, x * MY, MY, 0)
-
-    position = (d % PLACES) * COLS + jnp.arange(COLS)
-    ranks = jnp.tile(rank, 128)
-    my_rank = lax.dynamic_slice_in_dim(jnp.tile(rank, 20), (d * COLS) % O, COLS, 0)
-    a_slot = 2 * (position // O - ((d % PLACES) * COLS) // O) + my_rank
-    a_code = SLOTS * a_sym + a_slot
-    a_code = jnp.pad(a_code, (0, APAD - COLS), constant_values=-1)
-    before = jnp.arange(BJ)[None, :] < jnp.arange(BJ)[:, None]
-    bj_slot = jnp.sum(((bj_sym[:, None] == bj_sym[None, :]) & before).astype(I32), axis=1)
-    bj_code = jnp.pad(8 * bj_sym + bj_slot, (0, BPAD - BJ), constant_values=-1)
-    rank_key = 2 * (jnp.arange(2048) // O) + ranks
-
-    def pad(v, size, value):
-        return jnp.pad(v, (0, size - v.shape[0]), constant_values=value)
-
     vmem = pl.BlockSpec(memory_space=pltpu.VMEM)
     hbm = pl.BlockSpec(memory_space=pl.ANY)
     out = pl.pallas_call(
         kernel,
         out_shape=jax.ShapeDtypeStruct((BJ, MY), F32),
-        in_specs=[hbm, hbm] + [vmem] * 11,
+        in_specs=[hbm, hbm] + [vmem] * 5,
         out_specs=vmem,
         scratch_shapes=[
             pltpu.VMEM((COLS, ROWS), F32),
@@ -338,6 +404,7 @@
             pltpu.VMEM((PLACES, SLOTS, 384), F32),
             pltpu.VMEM((2 * Z, 8, 384), F32),
             pltpu.VMEM((384, 384), F32),
+            pltpu.VMEM((1, 38 * 128), I32),
             pltpu.VMEM((X, 2 * Z, 8, 128), F32),
             pltpu.VMEM((Z * PLACES, 8, 128), F32),
             pltpu.SemaphoreType.DMA((2,)),
@@ -356,17 +423,11 @@
     )(
         amplitudes.T,
         integrals,
-        row_sym[None, :],
-        a_sym[:, None],
-        w_sym[None, :],
-        pad(bj_sym, BPAD, -1)[:, None],
-        jnp.concatenate([a_code, a_code])[None, :],
-        jnp.concatenate([bj_code, bj_code])[None, :],
-        bj_code[:, None],
-        rank_key[None, :],
-        out_sym[None, :],
-        out_shift[None, :],
-        pad(bj_shift, BPAD, 1.0)[:, None],
+        slab_irrep,
+        virtual_irrep,
+        occupied_irrep,
+        occupied_energy,
+        slab_energy,
     )
     return out.T
 

time: 42.6 us -> 40.8 us (0.958)
  other arithmetic: 3.9 us -> 0 us
  local copies, waits for them, and re-layouts: 3.34 us -> 5.21 us
    unnamed x3 -> x13, local copies, waits for them, and re-layouts: 1.84 us -> 5.21 us
    xor x2 -> x0, other arithmetic: 1.71 us -> none  [the longest x1 0.93 us: local(): col_sym = (virtual_irrep[:, None] ^ occupied_irrep[None, :]).reshape(-1)]
    reduce_sum x2 -> x0, other arithmetic: 1.09 us -> none  [the longest x1 0.91 us: local(): rank = jnp.sum((same & earlier).astype(I32), axis=1)]
    sub x1 -> x0, other arithmetic: 0.77 us -> none  [local(): shifts = (occupied_energy[None, :] - slab_energy[:, None]).reshape(-1)]
    broadcast_in_dim x11 -> x0, local copies, waits for them, and re-layouts: 0.43 us -> none  [the longest x2 0.1 us: local(): pad(bj_shift, BPAD, 1.0)[:, None]]
where the time goes in v3:
time: 40.8 us; the launch traced here: 40.6 us
  Pallas kernels  35.4 us (87%)
  local copies, waits for them, and re-layouts  5.21 us (13%)
    pallas_call x1, Pallas kernels, local(): pl.pallas_call(kernel, out_shape=jax.ShapeDtypeStruct((BJ, MY), F32), in_...  35.4 us
    unnamed x13, local copies, waits for them, and re-layouts  5.21 us

profile of v3, /device:TPU:1, one launch (start us, length us, event | category | flops | bytes accessed | tf_op | source)
XLA Modules:
  0.0 40.6 jit_solution(6828096509223773938)
XLA Ops:
  0.0 0.0 copy-start
  0.0 1.2 %copy-done = f32[44,4800]{1,0:T(8,128)S(1)} copy-done((f32[44,4800]{1,0:T(8,128)S(1)}, f32[44,4800]{1,0:T(8,128)}, u32[]{:S(2)}) %copy-start) | copy-done | bytes 844824
  1.2 0.0 copy-start.1
  1.2 0.7 %copy-done.1 = s32[1200]{0:T(1024)S(1)} copy-done((s32[1200]{0:T(1024)S(1)}, s32[1200]{0:T(1024)}, u32[]{:S(2)}) %copy-start.1) | copy-done | bytes 4824
  1.9 0.0 copy-start.2
  1.9 0.7 %copy-done.2 = s32[176]{0:T(256)S(1)} copy-done((s32[176]{0:T(256)S(1)}, s32[176]{0:T(256)}, u32[]{:S(2)}) %copy-start.2) | copy-done | bytes 728
  2.6 0.0 copy-start.3
  2.6 0.7 %copy-done.3 = f32[176]{0:T(256)S(1)} copy-done((f32[176]{0:T(256)S(1)}, f32[176]{0:T(256)}, u32[]{:S(2)}) %copy-start.3) | copy-done | bytes 728
  3.2 0.0 copy-start.4
  3.2 0.7 %copy-done.4 = s32[16]{0:T(128)S(1)} copy-done((s32[16]{0:T(128)S(1)}, s32[16]{0:T(128)}, u32[]{:S(2)}) %copy-start.4) | copy-done | bytes 88
  3.9 0.0 copy-start.5
  3.9 0.7 %copy-done.5 = f32[16]{0:T(128)S(1)} copy-done((f32[16]{0:T(128)S(1)}, f32[16]{0:T(128)}, u32[]{:S(2)}) %copy-start.5) | copy-done | bytes 88
  4.6 35.4 %shard_map.73 = f32[44,704]{1,0:T(8,128)S(1)} custom-call(f32[300,2816]{1,0:T(8,128)} %bitcast.3, f32[44,4800]{1,0:T(8,128)S(1)} %copy-done, s32[176]{0:T(256)S(1)} %copy-done.2, s32[1200]{0:T(1024)S(1)} %copy-done.1, s32[16]{0:T(128)S(1)} %copy-done.4, f32[16]{0:T(128)S(1)} %copy-done.5, f32[176]{0:T(256)S(1)} %copy-done.3), custom_call_target="tpu_custom_call" | custom-call | tf_op jit(solution)/shard_map/pallas_call | solution.py:390
  39.9 0.7 %copy.9 = f32[704,44]{0,1:T(8,128)} copy(f32[704,44]{0,1:T(8,128)S(1)} %bitcast.2) | data formatting | bytes 247808
Async XLA Ops:
  0.0 1.2 %copy-start = (f32[44,4800]{1,0:T(8,128)S(1)}, f32[44,4800]{1,0:T(8,128)}, u32[]{:S(2)}) copy-start(f32[44,4800]{1,0:T(8,128)} %w_hbm.1) | copy-start | bytes 2534404
  1.2 0.7 %copy-start.1 = (s32[1200]{0:T(1024)S(1)}, s32[1200]{0:T(1024)}, u32[]{:S(2)}) copy-start(s32[1200]{0:T(1024)} %virtual_ref.1) | copy-start | bytes 14404
  1.9 0.7 %copy-start.2 = (s32[176]{0:T(256)S(1)}, s32[176]{0:T(256)}, u32[]{:S(2)}) copy-start(s32[176]{0:T(256)} %slab_ref.1) | copy-start | bytes 2116
  2.6 0.7 %copy-start.3 = (f32[176]{0:T(256)S(1)}, f32[176]{0:T(256)}, u32[]{:S(2)}) copy-start(f32[176]{0:T(256)} %slab_energy_ref.1) | copy-start | bytes 2116
  3.2 0.7 %copy-start.4 = (s32[16]{0:T(128)S(1)}, s32[16]{0:T(128)}, u32[]{:S(2)}) copy-start(s32[16]{0:T(128)} %occupied_ref.1) | copy-start | bytes 196
  3.9 0.7 %copy-start.5 = (f32[16]{0:T(128)S(1)}, f32[16]{0:T(128)}, u32[]{:S(2)}) copy-start(f32[16]{0:T(128)} %occupied_energy_ref.1) | copy-start | bytes 196

commit v4 on v3

--- a/solution.py
+++ b/solution.py
@@ -70,12 +70,17 @@
 def kernel(
     a_hbm,
     w_hbm,
+    slab_hbm,
+    virtual_hbm,
+    occupied_hbm,
+    occupied_energy_hbm,
+    slab_energy_hbm,
+    out_ref,
     slab_ref,
     virtual_ref,
     occupied_ref,
     occupied_energy_ref,
     slab_energy_ref,
-    out_ref,
     a_in,
     w_in,
     a_split,
@@ -106,6 +111,20 @@
     y, core = place // 2, place % 2
     load_a = pltpu.make_async_copy(a_hbm, a_in, load_sem.at[0])
     load_w = pltpu.make_async_copy(w_hbm, w_in, load_sem.at[1])
+    loads = [
+        pltpu.make_async_copy(source, target, load_sem.at[2 + n])
+        for n, (source, target) in enumerate(
+            [
+                (occupied_hbm, occupied_ref),
+                (slab_hbm, slab_ref),
+                (virtual_hbm, virtual_ref),
+                (occupied_energy_hbm, occupied_energy_ref),
+                (slab_energy_hbm, slab_energy_ref),
+            ]
+        )
+    ]
+    for load in loads:
+        load.start()
     load_w.start()
     load_a.start()
 
@@ -126,6 +145,8 @@
     lax.fori_loop(2 - core, PLACES - core, greet_a, 0)
     lax.fori_loop(1, Z * PLACES, greet_o, 0)
 
+    for load in loads:
+        load.wait()
     slab = slab_ref[...].reshape(1, -1).astype(F32)
     virtual = virtual_ref[...].reshape(1, -1).astype(F32)
     occupied = occupied_ref[...].reshape(1, -1).astype(F32)
@@ -386,13 +407,18 @@
     amplitudes, integrals, slab_irrep, virtual_irrep, occupied_irrep, occupied_energy, slab_energy
 ):
     vmem = pl.BlockSpec(memory_space=pltpu.VMEM)
-    hbm = pl.BlockSpec(memory_space=pl.ANY)
+    hbm = pl.BlockSpec(memory_space=pltpu.HBM)
     out = pl.pallas_call(
         kernel,
         out_shape=jax.ShapeDtypeStruct((BJ, MY), F32),
-        in_specs=[hbm, hbm] + [vmem] * 5,
+        in_specs=[hbm] * 7,
         out_specs=vmem,
         scratch_shapes=[
+            pltpu.VMEM(slab_irrep.shape, I32),
+            pltpu.VMEM(virtual_irrep.shape, I32),
+            pltpu.VMEM(occupied_irrep.shape, I32),
+            pltpu.VMEM(occupied_energy.shape, F32),
+            pltpu.VMEM(slab_energy.shape, F32),
             pltpu.VMEM((COLS, ROWS), F32),
             pltpu.VMEM((BJ, WIDE), F32),
             pltpu.VMEM((2 * APAD, ROWS), BF16),
@@ -407,7 +433,7 @@
             pltpu.VMEM((1, 38 * 128), I32),
             pltpu.VMEM((X, 2 * Z, 8, 128), F32),
             pltpu.VMEM((Z * PLACES, 8, 128), F32),
-            pltpu.SemaphoreType.DMA((2,)),
+            pltpu.SemaphoreType.DMA((7,)),
             pltpu.SemaphoreType.DMA((PLACES,)),
             pltpu.SemaphoreType.DMA((6,)),
             pltpu.SemaphoreType.DMA((2 * Z,)),
@@ -418,7 +444,7 @@
             pltpu.SemaphoreType.DMA,
         ],
         compiler_params=pltpu.CompilerParams(
-            collective_id=0, has_side_effects=True, vmem_limit_bytes=52 * 1024 * 1024
+            collective_id=0, has_side_effects=True, vmem_limit_bytes=58 << 20
         ),
     )(
         amplitudes.T,

time: 40.8 us -> 37.5 us (0.919)
  local copies, waits for them, and re-layouts: 5.21 us -> 1.58 us
    unnamed x13 -> x1, local copies, waits for them, and re-layouts: 5.21 us -> 1.58 us
    pallas_call x1, Pallas kernels: 35.4 us -> 35.8 us  [local(): pl.pallas_call(kernel, out_shape=jax.ShapeDtypeStruct((BJ, MY), F32), in_...]
where the time goes in v4:
time: 37.5 us; the launch traced here: 37.4 us
  Pallas kernels  35.8 us (95%)
  local copies, waits for them, and re-layouts  1.58 us (4%)
    pallas_call x1, Pallas kernels, local(): pl.pallas_call(kernel, out_shape=jax.ShapeDtypeStruct((BJ, MY), F32), in_...  35.8 us
    unnamed x1, local copies, waits for them, and re-layouts  1.58 us

profile of v4, /device:TPU:1, one launch (start us, length us, event | category | flops | bytes accessed | tf_op | source)
XLA Modules:
  0.0 37.4 jit_solution(12483947922542982803)
XLA Ops:
  0.0 35.8 %shard_map.73 = f32[44,704]{1,0:T(8,128)} custom-call(f32[300,2816]{1,0:T(8,128)} %bitcast.2, f32[44,4800]{1,0:T(8,128)} %w_hbm.1, s32[176]{0:T(256)} %slab_hbm.1, s32[1200]{0:T(1024)} %virtual_hbm.1, s32[16]{0:T(128)} %occupied_hbm.1, f32[16]{0:T(128)} %occupied_energy_hbm.1, f32[176]{0:T(256)} %slab_energy_hbm.1), custom_call_target="tpu_custom_call" | custom-call | tf_op jit(solution)/shard_map/pallas_call | solution.py:411
  35.8 1.6 %copy.9 = f32[704,44]{0,1:T(8,128)} copy(f32[704,44]{0,1:T(8,128)} %bitcast.3) | data formatting | bytes 247808

commit v5 on v4

--- a/solution.py
+++ b/solution.py
@@ -61,6 +61,9 @@
     parts = jnp.where((at >> 3) == iota((count, size), 0), values, 0.0)
     spread = ((iota((size, 128), 0) - offset) & 7) == (iota((size, 128), 1) >> 4)
     return parts, spread
+
+
+FAR_FIRST = (4, 5, 3, 6, 2, 7, 1, 0)
 
 
 def side_by_side(rows, first, count):
@@ -107,8 +110,13 @@
 ):
     d = lax.axis_index("dist")
     x = lax.axis_index("rep")
-    z, place = d // PLACES, d % PLACES
-    y, core = place // 2, place % 2
+    z, place = lax.div(d, PLACES), lax.rem(d, PLACES)
+    y, core = lax.div(place, 2), lax.rem(place, 2)
+    z_at = [lax.rem(z + n, Z) for n in range(Z)]
+    y_at = [lax.rem(y + n, Y) for n in range(Y)]
+    x_at = [lax.rem(x + n, X) for n in range(X)]
+    core_at = [core, 1 - core]
+    here = y * 2
     load_a = pltpu.make_async_copy(a_hbm, a_in, load_sem.at[0])
     load_w = pltpu.make_async_copy(w_hbm, w_in, load_sem.at[1])
     loads = [
@@ -133,17 +141,14 @@
     def greet(dd, xx):
         pl.semaphore_signal(barrier, inc=1, device_id=(dd, xx), device_id_type=MESH)
 
-    def greet_a(i, carry):
-        greet(z * PLACES + (place + i) % PLACES, x)
-        return carry
-
-    def greet_o(i, carry):
-        zs, cs, xs = (z + i // PLACES) % Z, (core + i) % 2, (x + (i % PLACES) // 2) % X
-        greet(zs * PLACES + y * 2 + cs, xs)
-        return carry
-
-    lax.fori_loop(2 - core, PLACES - core, greet_a, 0)
-    lax.fori_loop(1, Z * PLACES, greet_o, 0)
+    for n in FAR_FIRST:
+        for m in range(X):
+            for j in range(2):
+                if n or m or j:
+                    greet(z_at[n] * PLACES + here + core_at[j], x_at[m])
+    for m in range(1, Y):
+        for j in range(2):
+            greet(z * PLACES + y_at[m] * 2 + core_at[j], x)
 
     for load in loads:
         load.wait()
@@ -226,7 +231,7 @@
     for n in range(16):
         pick[:, pl.ds(n * 128, 128)] = small(key + 16 * n == iota((256, 128), 0))
     for n in range(4):
-        o_msg[n] = jnp.zeros((2 * Z, 8, 128), F32)
+        o_msg[n] = jnp.zeros((2, Z, 8, 128), F32)
         w_split[pl.ds(n * BPAD + 32, 16)] = jnp.zeros((16, 2432), BF16)
     for n in range(2):
         a_split[pl.ds(n * APAD + 288, 16)] = jnp.zeros((16, ROWS), BF16)
@@ -249,27 +254,6 @@
         rest = sum(matmul(group, w_rest[r].astype(BF16), NN) for r in rows)
         w_msg[:, half, :, pl.ds(0, 256)] = main.reshape(IRREPS, 8, 256)
         w_msg[:, half, :, pl.ds(256, 128)] = rest.reshape(IRREPS, 8, 128)
-
-    pl.semaphore_wait(barrier, 6 + Z * PLACES - 1)
-
-    def x_copy(i):
-        cs, xs = (core + i // 3) % 2, (x + 1 + i % 3) % X
-        return pltpu.make_async_remote_copy(
-            src_ref=w_msg.at[2 * xs + cs],
-            dst_ref=w_mid.at[cs, x],
-            send_sem=x_send.at[i],
-            recv_sem=x_recv.at[cs],
-            device_id=(d, xs),
-            device_id_type=MESH,
-        )
-
-    def send_x(i, carry):
-        x_copy(i).start()
-        return carry
-
-    lax.fori_loop(0, 6, send_x, 0)
-    for cs in range(2):
-        pltpu.make_async_copy(w_msg.at[2 * x + cs], w_mid.at[cs, x], x_recv.at[cs]).start()
 
     load_a.wait()
     for n in range(11):
@@ -291,82 +275,98 @@
     a_msg[:, :, pl.ds(0, 256)] = main.reshape(2, SLOTS, 256)
     a_msg[:, :, pl.ds(256, 128)] = rest.reshape(2, SLOTS, 128)
 
-    def a_copy(i):
-        to = (place + i) % PLACES
-        return pltpu.make_async_remote_copy(
-            src_ref=a_msg.at[to % 2],
-            dst_ref=a_got.at[place],
-            send_sem=a_send.at[i],
-            recv_sem=a_recv,
-            device_id=(z * PLACES + to, x),
+    pl.semaphore_wait(barrier, 6 + Z * PLACES - 1)
+
+    sends = []
+
+    def send(source, target, send_sem, recv_sem, dd, xx):
+        copy = pltpu.make_async_remote_copy(
+            src_ref=source,
+            dst_ref=target,
+            send_sem=send_sem,
+            recv_sem=recv_sem,
+            device_id=(dd, xx),
             device_id_type=MESH,
         )
-
-    def send_a(i, carry):
-        a_copy(i).start()
-        return carry
-
-    lax.fori_loop(1, PLACES, send_a, 0)
+        copy.start()
+        sends.append(copy)
+
+    for j in range(2):
+        cs = core_at[j]
+        for m in (2, 1, 3):
+            send(
+                w_msg.at[2 * x_at[m] + cs],
+                w_mid.at[cs, x],
+                x_send.at[3 * j + m - 1],
+                x_recv.at[cs],
+                d,
+                x_at[m],
+            )
+        pltpu.make_async_copy(w_msg.at[2 * x + cs], w_mid.at[cs, x], x_recv.at[cs]).start()
+
+    for m in (2, 1, 3, 0):
+        for j in range(2):
+            if m or j:
+                send(
+                    a_msg.at[core_at[j]],
+                    a_got.at[place],
+                    a_send.at[2 * m + j],
+                    a_recv,
+                    z * PLACES + y_at[m] * 2 + core_at[j],
+                    x,
+                )
     pltpu.make_async_copy(a_msg.at[core], a_got.at[place], a_recv).start()
 
-    slot_w = z * 2 + core
-
-    def w_copy(i):
-        cs, zs = (core + i // Z) % 2, (z + i) % Z
-        return pltpu.make_async_remote_copy(
-            src_ref=w_mid.at[cs, zs // 2, zs % 2],
-            dst_ref=w_got.at[slot_w],
-            send_sem=w_send.at[i],
-            recv_sem=w_recv,
-            device_id=(zs * PLACES + y * 2 + cs, x),
-            device_id_type=MESH,
-        )
-
-    def send_w(i, carry):
-        w_copy(i).start()
-        return carry
-
-    first, second = w_mid.at[core], w_mid.at[1 - core]
-    pltpu.make_async_copy(first, first, x_recv.at[core]).wait()
-    pltpu.make_async_copy(first.at[z // 2, z % 2], w_got.at[slot_w], w_recv).start()
-    lax.fori_loop(1, Z, send_w, 0)
-    pltpu.make_async_copy(second, second, x_recv.at[1 - core]).wait()
-    lax.fori_loop(Z, 2 * Z, send_w, 0)
+    for j in range(2):
+        ready = w_mid.at[core_at[j]]
+        pltpu.make_async_copy(ready, ready, x_recv.at[core_at[j]]).wait()
+        for n in FAR_FIRST:
+            zs = z_at[n]
+            if n or j:
+                send(
+                    ready.at[lax.div(zs, 2), lax.rem(zs, 2)],
+                    w_got.at[j, z],
+                    w_send.at[j, n],
+                    w_recv.at[j],
+                    zs * PLACES + here + core_at[j],
+                    x,
+                )
+            else:
+                pltpu.make_async_copy(
+                    ready.at[lax.div(z, 2), lax.rem(z, 2)], w_got.at[0, z], w_recv.at[0]
+                ).start()
 
     a_all[...] = jnp.zeros(a_all.shape, F32)
     pltpu.make_async_copy(a_got, a_got, a_recv).wait()
     for p in range(PLACES):
         first = 2 * START[p]
         a_all[pl.ds(first, SLOTS), :] += a_got[p]
-    pltpu.make_async_copy(w_got, w_got, w_recv).wait()
-    w_high, w_low = halves(w_got[...].reshape(2 * Z * 8, 384))
     a_high, a_low = halves(a_all[...])
-    product = matmul(w_high, a_low, NN) + matmul(w_low, a_high, NN)
-    product = product + matmul(w_high, a_high, NN)
-    for part in range(X):
-        o_msg[part, :, :, pl.ds(0, QA)] = product[:, part * QA : (part + 1) * QA].reshape(
-            2 * Z, 8, QA
-        )
-
-    def o_copy(i):
-        zs, cs, part = (z + i // PLACES) % Z, (core + i) % 2, (x + (i % PLACES) // 2) % X
-        return pltpu.make_async_remote_copy(
-            src_ref=o_msg.at[part, zs * 2 + cs],
-            dst_ref=o_got.at[z * PLACES + 2 * x + core],
-            send_sem=o_send.at[i],
-            recv_sem=o_recv,
-            device_id=(zs * PLACES + y * 2 + cs, part),
-            device_id_type=MESH,
-        )
-
-    def send_o(i, carry):
-        o_copy(i).start()
-        return carry
-
-    lax.fori_loop(1, Z * PLACES, send_o, 0)
-    pltpu.make_async_copy(
-        o_msg.at[x, slot_w], o_got.at[z * PLACES + 2 * x + core], o_recv
-    ).start()
+    slot_o = z * PLACES + 2 * x + core
+
+    for j in range(2):
+        pltpu.make_async_copy(w_got.at[j], w_got.at[j], w_recv.at[j]).wait()
+        w_high, w_low = halves(w_got[j].reshape(Z * 8, 384))
+        product = matmul(w_high, a_low, NN) + matmul(w_low, a_high, NN)
+        product = product + matmul(w_high, a_high, NN)
+        for part in range(X):
+            o_msg[part, j, :, :, pl.ds(0, QA)] = product[:, part * QA : (part + 1) * QA].reshape(
+                Z, 8, QA
+            )
+
+        for n in FAR_FIRST:
+            for m in range(X):
+                if n or m or j:
+                    send(
+                        o_msg.at[x_at[m], j, z_at[n]],
+                        o_got.at[slot_o],
+                        o_send.at[j, X * n + m],
+                        o_recv,
+                        z_at[n] * PLACES + here + core_at[j],
+                        x_at[m],
+                    )
+                else:
+                    pltpu.make_async_copy(o_msg.at[x, 0, z], o_got.at[slot_o], o_recv).start()
 
     spread = small((iota((BPAD, 128), 1) & 63) == bj_code_col)
     pltpu.make_async_copy(o_got, o_got, o_recv).wait()
@@ -381,26 +381,8 @@
     value = jnp.where(bj_sym == out_sym, cycle, 0.0) / (out_shift + bj_shift)
     out_ref[...] = value[:BJ]
 
-    def done_x(i, carry):
-        x_copy(i).wait_send()
-        return carry
-
-    def done_w(i, carry):
-        w_copy(i).wait_send()
-        return carry
-
-    def done_a(i, carry):
-        a_copy(i).wait_send()
-        return carry
-
-    def done_o(i, carry):
-        o_copy(i).wait_send()
-        return carry
-
-    lax.fori_loop(0, 6, done_x, 0)
-    lax.fori_loop(1, 2 * Z, done_w, 0)
-    lax.fori_loop(1, PLACES, done_a, 0)
-    lax.fori_loop(1, Z * PLACES, done_o, 0)
+    for copy in sends:
+        copy.wait_send()
 
 
 def local(
@@ -428,19 +410,19 @@
             pltpu.VMEM((IRREPS, 2, 8, 384), F32),
             pltpu.VMEM((2, X, 2, 8, 384), F32),
             pltpu.VMEM((PLACES, SLOTS, 384), F32),
-            pltpu.VMEM((2 * Z, 8, 384), F32),
+            pltpu.VMEM((2, Z, 8, 384), F32),
             pltpu.VMEM((384, 384), F32),
             pltpu.VMEM((1, 38 * 128), I32),
-            pltpu.VMEM((X, 2 * Z, 8, 128), F32),
+            pltpu.VMEM((X, 2, Z, 8, 128), F32),
             pltpu.VMEM((Z * PLACES, 8, 128), F32),
             pltpu.SemaphoreType.DMA((7,)),
             pltpu.SemaphoreType.DMA((PLACES,)),
             pltpu.SemaphoreType.DMA((6,)),
-            pltpu.SemaphoreType.DMA((2 * Z,)),
-            pltpu.SemaphoreType.DMA((Z * PLACES,)),
+            pltpu.SemaphoreType.DMA((2, Z)),
+            pltpu.SemaphoreType.DMA((2, Z * X)),
             pltpu.SemaphoreType.DMA,
             pltpu.SemaphoreType.DMA((2,)),
-            pltpu.SemaphoreType.DMA,
+            pltpu.SemaphoreType.DMA((2,)),
             pltpu.SemaphoreType.DMA,
         ],
         compiler_params=pltpu.CompilerParams(

time: 37.5 us -> 34.2 us (0.912)
  Pallas kernels: 35.8 us -> 32.5 us
    pallas_call x1, Pallas kernels: 35.8 us -> 32.5 us  [local(): pl.pallas_call(kernel, out_shape=jax.ShapeDtypeStruct((BJ, MY), F32), in_...]
where the time goes in v5:
time: 34.2 us; the launch traced here: 34.1 us
  Pallas kernels  32.5 us (95%)
  local copies, waits for them, and re-layouts  1.58 us (5%)
    pallas_call x1, Pallas kernels, local(): pl.pallas_call(kernel, out_shape=jax.ShapeDtypeStruct((BJ, MY), F32), in_...  32.5 us
    unnamed x1, local copies, waits for them, and re-layouts  1.58 us

profile of v5, /device:TPU:1, one launch (start us, length us, event | category | flops | bytes accessed | tf_op | source)
XLA Modules:
  0.0 34.1 jit_solution(2002506901183898818)
XLA Ops:
  0.0 32.5 %shard_map.73 = f32[44,704]{1,0:T(8,128)} custom-call(f32[300,2816]{1,0:T(8,128)} %bitcast.2, f32[44,4800]{1,0:T(8,128)} %w_hbm.1, s32[176]{0:T(256)} %slab_hbm.1, s32[1200]{0:T(1024)} %virtual_hbm.1, s32[16]{0:T(128)} %occupied_hbm.1, f32[16]{0:T(128)} %occupied_energy_hbm.1, f32[176]{0:T(256)} %slab_energy_hbm.1), custom_call_target="tpu_custom_call" | custom-call | tf_op jit(solution)/shard_map/pallas_call | solution.py:393
  32.5 1.6 %copy.9 = f32[704,44]{0,1:T(8,128)} copy(f32[704,44]{0,1:T(8,128)} %bitcast.3) | data formatting | bytes 247808

commit v6 on v5

--- a/solution.py
+++ b/solution.py
@@ -98,6 +98,7 @@
     w_sym,
     o_msg,
     o_got,
+    o_sum,
     load_sem,
     a_send,
     x_send,
@@ -231,7 +232,6 @@
     for n in range(16):
         pick[:, pl.ds(n * 128, 128)] = small(key + 16 * n == iota((256, 128), 0))
     for n in range(4):
-        o_msg[n] = jnp.zeros((2, Z, 8, 128), F32)
         w_split[pl.ds(n * BPAD + 32, 16)] = jnp.zeros((16, 2432), BF16)
     for n in range(2):
         a_split[pl.ds(n * APAD + 288, 16)] = jnp.zeros((16, ROWS), BF16)
@@ -247,13 +247,19 @@
     w_rest = matmul(
         w_split[:, pl.ds(2048, HALF - 2048)], pick[pl.ds(0, 128), pl.ds(0, HALF - 2048)], NT
     )
-    group = small(iota((IRREPS * 8, BPAD), 0) == bj_code)
+    row = iota((IRREPS * 8, BPAD), 0)
+    group = small(row == bj_code)
+    row = row & 31
+    row = 8 * (row >> 2) + (row & 3) + 4 * (iota((IRREPS * 8, BPAD), 0) >> 5)
+    group_rest = small(row == bj_code)
     for half in range(2):
         rows = [slice((2 * half + n) * BPAD, (2 * half + n + 1) * BPAD) for n in range(2)]
         main = sum(matmul(group, w_main[r].astype(BF16), NN) for r in rows)
-        rest = sum(matmul(group, w_rest[r].astype(BF16), NN) for r in rows)
-        w_msg[:, half, :, pl.ds(0, 256)] = main.reshape(IRREPS, 8, 256)
-        w_msg[:, half, :, pl.ds(256, 128)] = rest.reshape(IRREPS, 8, 128)
+        rest = sum(matmul(group_rest, w_rest[r].astype(BF16), NN) for r in rows)
+        w_msg[:, half, pl.ds(0, 8)] = main[:, :128].reshape(IRREPS, 8, 128)
+        w_msg[:, half, pl.ds(8, 8)] = main[:, 128:].reshape(IRREPS, 8, 128)
+        rest = rest[:32] + pltpu.roll(rest[32:], 64, 1)
+        w_msg[:, half, pl.ds(16, 4)] = rest.reshape(IRREPS, 4, 128)
 
     load_a.wait()
     for n in range(11):
@@ -346,13 +352,36 @@
 
     for j in range(2):
         pltpu.make_async_copy(w_got.at[j], w_got.at[j], w_recv.at[j]).wait()
-        w_high, w_low = halves(w_got[j].reshape(Z * 8, 384))
+        rows = []
+        for slot in range(8):
+            tail = w_got[j, :, 16 + slot % 4, :]
+            if slot >= 4:
+                tail = pltpu.roll(tail, 64, 1)
+            rows.append(
+                jnp.concatenate([w_got[j, :, slot, :], w_got[j, :, 8 + slot, :], tail], axis=1)
+            )
+        w_high, w_low = halves(jnp.concatenate(rows, axis=0))
         product = matmul(w_high, a_low, NN) + matmul(w_low, a_high, NN)
         product = product + matmul(w_high, a_high, NN)
         for part in range(X):
-            o_msg[part, j, :, :, pl.ds(0, QA)] = product[:, part * QA : (part + 1) * QA].reshape(
-                Z, 8, QA
-            )
+            lanes = product[:, part * QA : (part + 1) * QA]
+            ends = []
+            for slot in (6, 7):
+                whole = lanes[8 * slot : 8 * slot + 8]
+                ends.append([whole[:, :40], whole[:, 40:80], whole[:, 80:]])
+            nothing = jnp.zeros((8, 32), F32)
+            ends = [
+                ends[0][0],
+                ends[0][1],
+                ends[1][0],
+                ends[1][1],
+                jnp.concatenate([ends[0][2], nothing], axis=1),
+                jnp.concatenate([ends[1][2], nothing], axis=1),
+            ]
+            for slot in range(6):
+                o_msg[part, j, :, slot, :] = jnp.concatenate(
+                    [lanes[8 * slot : 8 * slot + 8], ends[slot]], axis=1
+                )
 
         for n in FAR_FIRST:
             for m in range(X):
@@ -368,13 +397,29 @@
                 else:
                     pltpu.make_async_copy(o_msg.at[x, 0, z], o_got.at[slot_o], o_recv).start()
 
-    spread = small((iota((BPAD, 128), 1) & 63) == bj_code_col)
+    o_sum[...] = jnp.zeros(o_sum.shape, F32)
+    source = iota((BPAD, 128), 1) & 63
+    spread = small(source == bj_code_col)
+    end_row = source & 7
+    end_slot = jnp.where((end_row == 2) | (end_row == 3) | (end_row == 5), 7, 6)
+    end_slot = jnp.where(end_row < 6, end_slot, 8)
+    spread_ends = small((source & 56) + end_slot == bj_code_col)
     pltpu.make_async_copy(o_got, o_got, o_recv).wait()
     total = o_got[pl.ds(0, PLACES)]
     for zs in range(1, Z):
         total = total + o_got[pl.ds(zs * PLACES, PLACES)]
-    high, low = halves(total.reshape(IRREPS * 8, 128))
+    o_sum[:, pl.ds(0, 6), :] = total
+    total = o_sum[...].reshape(IRREPS * 8, 128)
+    row, lane = iota((IRREPS * 8, 128), 0) & 7, iota((IRREPS * 8, 128), 1)
+    first = jnp.where(((row == 0) | (row == 2)) & (lane < 40), pltpu.roll(total, 40, 1), 0.0)
+    second = ((row == 1) | (row == 3)) & (lane >= 40) & (lane < 80)
+    second = jnp.where(second, pltpu.roll(total, 80, 1), 0.0)
+    third = ((row == 4) | (row == 5)) & (lane >= 80) & (lane < QA)
+    third = jnp.where(third, pltpu.roll(total, 120, 1), 0.0)
+    high, low = halves(total)
     mine = matmul(spread, jnp.concatenate([high, low], axis=0), NN)
+    high, low = halves(first + second + third)
+    mine = mine + matmul(spread_ends, jnp.concatenate([high, low], axis=0), NN)
     high, low = halves(mine)
     widen = pick[pl.ds(0, 128), pl.ds(0, MY)]
     cycle = matmul(high, widen, NN) + matmul(low, widen, NN)
@@ -407,14 +452,15 @@
             pltpu.VMEM((4 * BPAD, 2432), BF16),
             pltpu.VMEM((256, 2048), BF16),
             pltpu.VMEM((2, SLOTS, 384), F32),
-            pltpu.VMEM((IRREPS, 2, 8, 384), F32),
-            pltpu.VMEM((2, X, 2, 8, 384), F32),
+            pltpu.VMEM((IRREPS, 2, 20, 128), F32),
+            pltpu.VMEM((2, X, 2, 20, 128), F32),
             pltpu.VMEM((PLACES, SLOTS, 384), F32),
-            pltpu.VMEM((2, Z, 8, 384), F32),
+            pltpu.VMEM((2, Z, 20, 128), F32),
             pltpu.VMEM((384, 384), F32),
             pltpu.VMEM((1, 38 * 128), I32),
-            pltpu.VMEM((X, 2, Z, 8, 128), F32),
-            pltpu.VMEM((Z * PLACES, 8, 128), F32),
+            pltpu.VMEM((X, 2, Z, 6, 128), F32),
+            pltpu.VMEM((Z * PLACES, 6, 128), F32),
+            pltpu.VMEM((IRREPS, 8, 128), F32),
             pltpu.SemaphoreType.DMA((7,)),
             pltpu.SemaphoreType.DMA((PLACES,)),
             pltpu.SemaphoreType.DMA((6,)),

time: 34.2 us -> 33 us (0.965)
  Pallas kernels: 32.5 us -> 31.4 us
    pallas_call x1, Pallas kernels: 32.5 us -> 31.4 us  [local(): pl.pallas_call(kernel, out_shape=jax.ShapeDtypeStruct((BJ, MY), F32), in_...]
where the time goes in v6:
time: 33 us; the launch traced here: 32.9 us
  Pallas kernels  31.4 us (95%)
  local copies, waits for them, and re-layouts  1.58 us (5%)
    pallas_call x1, Pallas kernels, local(): pl.pallas_call(kernel, out_shape=jax.ShapeDtypeStruct((BJ, MY), F32), in_...  31.4 us
    unnamed x1, local copies, waits for them, and re-layouts  1.58 us

profile of v6, /device:TPU:1, one launch (start us, length us, event | category | flops | bytes accessed | tf_op | source)
XLA Modules:
  0.0 32.9 jit_solution(10205025657840599075)
XLA Ops:
  0.0 31.4 %shard_map.73 = f32[44,704]{1,0:T(8,128)} custom-call(f32[300,2816]{1,0:T(8,128)} %bitcast.2, f32[44,4800]{1,0:T(8,128)} %w_hbm.1, s32[176]{0:T(256)} %slab_hbm.1, s32[1200]{0:T(1024)} %virtual_hbm.1, s32[16]{0:T(128)} %occupied_hbm.1, f32[16]{0:T(128)} %occupied_energy_hbm.1, f32[176]{0:T(256)} %slab_energy_hbm.1), custom_call_target="tpu_custom_call" | custom-call | tf_op jit(solution)/shard_map/pallas_call | solution.py:438
  31.4 1.6 %copy.9 = f32[704,44]{0,1:T(8,128)} copy(f32[704,44]{0,1:T(8,128)} %bitcast.3) | data formatting | bytes 247808

commit v7 on v6

--- a/solution.py
+++ b/solution.py
@@ -104,6 +104,7 @@
     x_send,
     w_send,
     o_send,
+    a_first,
     a_recv,
     x_recv,
     w_recv,
@@ -164,7 +165,6 @@
 
     repeat = iota((O, 128), 0) == (iota((O, 128), 1) & 15)
     occ_lane = matmul(occ_all[:16], small(repeat), NN)[:1].astype(I32)
-    occ_energy_lane = exact(jnp.broadcast_to(occupied_energy, (8, O)), one_hot(repeat), NN)[:1]
     occ_col = matmul(small(iota((O, O), 0) == iota((O, O), 1)), occ_all, NT).astype(I32)
     earlier = (occ_col == occ_lane) & (iota((O, 128), 0) < (iota((O, 128), 1) & 15))
     rank = jnp.sum(one_hot(earlier), axis=0, keepdims=True)
@@ -172,13 +172,6 @@
 
     parts, spread = tiles(slab, 0, 32)
     row_sym = matmul(parts.astype(BF16), small(spread), NN).astype(I32) ^ occ_lane
-    parts, spread = tiles(slab, (MY // O) * x, 16)
-    out_sym = matmul(parts.astype(BF16), small(spread), NN).astype(I32) ^ occ_lane
-    parts, _ = tiles(slab_energy, (MY // O) * x, 8)
-    out_shift = occ_energy_lane - exact(parts, one_hot(spread), NN)
-    out_sym = side_by_side(out_sym, 0, 6)[:, :MY]
-    out_shift = side_by_side(out_shift, 0, 6)[:, :MY]
-
     parts, spread = tiles(virtual, (WIDE // O) * x, 48)
     columns = matmul(parts.astype(BF16), small(spread), NN).astype(I32) ^ occ_lane
     for n in range(38):
@@ -212,10 +205,6 @@
         small(pick_j), occ_all, NT
     ).astype(I32)
     bj_sym = jnp.where(iota((BPAD, 128), 0) < BJ, bj_col, -1)
-    bj_shift = (
-        exact(one_hot(pick_j), jnp.broadcast_to(occupied_energy, (128, O)), NT)
-        - exact(one_hot(pick_b), jnp.broadcast_to(slab_energy, (128, n_slab)), NT)
-    )[:, :1]
     at = BJ * d + iota((n_slab, 128), 1)
     b_row = matmul(slab_all[:16], small((at >> 4) == iota((n_slab, 128), 0)), NN)[:1]
     at = BJ * d + iota((O, 128), 1)
@@ -224,13 +213,13 @@
     same = bj_sym == bj_row
     shape = (BPAD, 128)
     slot_row = jnp.sum(one_hot(same & (iota(shape, 0) < iota(shape, 1))), axis=0, keepdims=True)
-    slot_col = jnp.sum(one_hot(same & (iota(shape, 1) < iota(shape, 0))), axis=1, keepdims=True)
     bj_code = jnp.where(bj_row < 0, -1, 8 * bj_row + slot_row.astype(I32))[:, :BPAD]
     bj_sym = bj_sym[:, :1]
-    bj_code_col = jnp.where(bj_sym < 0, -1, 8 * bj_sym + slot_col.astype(I32))
-
+
+    pick[...] = jnp.zeros(pick.shape, BF16)
+    one_tile = small(key == iota((16, 128), 0))
     for n in range(16):
-        pick[:, pl.ds(n * 128, 128)] = small(key + 16 * n == iota((256, 128), 0))
+        pick[pl.ds(16 * n, 16), pl.ds(n * 128, 128)] = one_tile
     for n in range(4):
         w_split[pl.ds(n * BPAD + 32, 16)] = jnp.zeros((16, 2432), BF16)
     for n in range(2):
@@ -310,18 +299,33 @@
             )
         pltpu.make_async_copy(w_msg.at[2 * x + cs], w_mid.at[cs, x], x_recv.at[cs]).start()
 
-    for m in (2, 1, 3, 0):
+    for m in (3, 1, 2, 0):
         for j in range(2):
-            if m or j:
+            if (m or j) and not (m == 2 and j):
                 send(
                     a_msg.at[core_at[j]],
                     a_got.at[place],
                     a_send.at[2 * m + j],
-                    a_recv,
+                    a_first if m == 3 and j else a_recv,
                     z * PLACES + y_at[m] * 2 + core_at[j],
                     x,
                 )
     pltpu.make_async_copy(a_msg.at[core], a_got.at[place], a_recv).start()
+
+    occ_energy_lane = exact(jnp.broadcast_to(occupied_energy, (8, O)), one_hot(repeat), NN)[:1]
+    parts, spread = tiles(slab, (MY // O) * x, 16)
+    out_sym = matmul(parts.astype(BF16), small(spread), NN).astype(I32) ^ occ_lane
+    parts, _ = tiles(slab_energy, (MY // O) * x, 8)
+    out_shift = occ_energy_lane - exact(parts, one_hot(spread), NN)
+    out_sym = side_by_side(out_sym, 0, 6)[:, :MY]
+    out_shift = side_by_side(out_shift, 0, 6)[:, :MY]
+
+    bj_shift = (
+        exact(one_hot(pick_j), jnp.broadcast_to(occupied_energy, (128, O)), NT)
+        - exact(one_hot(pick_b), jnp.broadcast_to(slab_energy, (128, n_slab)), NT)
+    )[:, :1]
+    slot_col = jnp.sum(one_hot(same & (iota(shape, 1) < iota(shape, 0))), axis=1, keepdims=True)
+    bj_code_col = jnp.where(bj_sym < 0, -1, 8 * bj_sym + slot_col.astype(I32))
 
     for j in range(2):
         ready = w_mid.at[core_at[j]]
@@ -342,8 +346,13 @@
                     ready.at[lax.div(z, 2), lax.rem(z, 2)], w_got.at[0, z], w_recv.at[0]
                 ).start()
 
+    passed = a_got.at[y_at[1] * 2 + core_at[1]]
+    pltpu.make_async_copy(passed, passed, a_first).wait()
+    send(passed, passed, a_send.at[5], a_recv, z * PLACES + y_at[3] * 2 + core, x)
+
     a_all[...] = jnp.zeros(a_all.shape, F32)
-    pltpu.make_async_copy(a_got, a_got, a_recv).wait()
+    others = a_got.at[pl.ds(0, PLACES - 1)]
+    pltpu.make_async_copy(others, others, a_recv).wait()
     for p in range(PLACES):
         first = 2 * START[p]
         a_all[pl.ds(first, SLOTS), :] += a_got[p]
@@ -467,6 +476,7 @@
             pltpu.SemaphoreType.DMA((2, Z)),
             pltpu.SemaphoreType.DMA((2, Z * X)),
             pltpu.SemaphoreType.DMA,
+            pltpu.SemaphoreType.DMA,
             pltpu.SemaphoreType.DMA((2,)),
             pltpu.SemaphoreType.DMA((2,)),
             pltpu.SemaphoreType.DMA,

time: 33 us -> 32 us (0.970)
  Pallas kernels: 31.4 us -> 30.3 us
    pallas_call x1, Pallas kernels: 31.4 us -> 30.3 us  [local(): pl.pallas_call(kernel, out_shape=jax.ShapeDtypeStruct((BJ, MY), F32), in_...]
where the time goes in v7:
time: 32 us; the launch traced here: 31.9 us
  Pallas kernels  30.3 us (95%)
  local copies, waits for them, and re-layouts  1.58 us (5%)
    pallas_call x1, Pallas kernels, local(): pl.pallas_call(kernel, out_shape=jax.ShapeDtypeStruct((BJ, MY), F32), in_...  30.3 us
    unnamed x1, local copies, waits for them, and re-layouts  1.58 us

profile of v7, /device:TPU:1, one launch (start us, length us, event | category | flops | bytes accessed | tf_op | source)
XLA Modules:
  0.0 31.9 jit_solution(17860244168860721113)
XLA Ops:
  0.0 30.3 %shard_map.73 = f32[44,704]{1,0:T(8,128)} custom-call(f32[300,2816]{1,0:T(8,128)} %bitcast.2, f32[44,4800]{1,0:T(8,128)} %w_hbm.1, s32[176]{0:T(256)} %slab_hbm.1, s32[1200]{0:T(1024)} %virtual_hbm.1, s32[16]{0:T(128)} %occupied_hbm.1, f32[16]{0:T(128)} %occupied_energy_hbm.1, f32[176]{0:T(256)} %slab_energy_hbm.1), custom_call_target="tpu_custom_call" | custom-call | tf_op jit(solution)/shard_map/pallas_call | solution.py:447
  30.4 1.6 %copy.9 = f32[704,44]{0,1:T(8,128)} copy(f32[704,44]{0,1:T(8,128)} %bitcast.3) | data formatting | bytes 247808

commit v8 on v7

--- a/solution.py
+++ b/solution.py
@@ -97,6 +97,7 @@
     a_all,
     w_sym,
     o_msg,
+    o_pass,
     o_got,
     o_sum,
     load_sem,
@@ -109,6 +110,8 @@
     x_recv,
     w_recv,
     o_recv,
+    pass_send,
+    pass_recv,
 ):
     d = lax.axis_index("dist")
     x = lax.axis_index("rep")
@@ -394,7 +397,16 @@
 
         for n in FAR_FIRST:
             for m in range(X):
-                if n or m or j:
+                if n == 4 and j == 0:
+                    send(
+                        o_msg.at[x_at[m], 0, z_at[n]],
+                        o_pass.at[m],
+                        o_send.at[0, X * n + m],
+                        pass_recv,
+                        z_at[7] * PLACES + here + core,
+                        x,
+                    )
+                elif n or m or j:
                     send(
                         o_msg.at[x_at[m], j, z_at[n]],
                         o_got.at[slot_o],
@@ -405,6 +417,17 @@
                     )
                 else:
                     pltpu.make_async_copy(o_msg.at[x, 0, z], o_got.at[slot_o], o_recv).start()
+
+    pltpu.make_async_copy(o_pass, o_pass, pass_recv).wait()
+    for m in range(X):
+        send(
+            o_pass.at[m],
+            o_got.at[z_at[1] * PLACES + 2 * x + core],
+            pass_send.at[m],
+            o_recv,
+            z_at[5] * PLACES + here + core,
+            x_at[m],
+        )
 
     o_sum[...] = jnp.zeros(o_sum.shape, F32)
     source = iota((BPAD, 128), 1) & 63
@@ -468,6 +491,7 @@
             pltpu.VMEM((384, 384), F32),
             pltpu.VMEM((1, 38 * 128), I32),
             pltpu.VMEM((X, 2, Z, 6, 128), F32),
+            pltpu.VMEM((X, 6, 128), F32),
             pltpu.VMEM((Z * PLACES, 6, 128), F32),
             pltpu.VMEM((IRREPS, 8, 128), F32),
             pltpu.SemaphoreType.DMA((7,)),
@@ -479,6 +503,8 @@
             pltpu.SemaphoreType.DMA,
             pltpu.SemaphoreType.DMA((2,)),
             pltpu.SemaphoreType.DMA((2,)),
+            pltpu.SemaphoreType.DMA,
+            pltpu.SemaphoreType.DMA((X,)),
             pltpu.SemaphoreType.DMA,
         ],
         compiler_params=pltpu.CompilerParams(

time: 32 us -> 31.5 us (0.984)
  Pallas kernels: 30.3 us -> 29.8 us
    pallas_call x1, Pallas kernels: 30.3 us -> 29.8 us  [local(): pl.pallas_call(kernel, out_shape=jax.ShapeDtypeStruct((BJ, MY), F32), in_...]
where the time goes in v8:
time: 31.5 us; the launch traced here: 31.4 us
  Pallas kernels  29.8 us (95%)
  local copies, waits for them, and re-layouts  1.58 us (5%)
    pallas_call x1, Pallas kernels, local(): pl.pallas_call(kernel, out_shape=jax.ShapeDtypeStruct((BJ, MY), F32), in_...  29.8 us
    unnamed x1, local copies, waits for them, and re-layouts  1.58 us

profile of v8, /device:TPU:1, one launch (start us, length us, event | category | flops | bytes accessed | tf_op | source)
XLA Modules:
  0.0 31.4 jit_solution(10931457473965000295)
XLA Ops:
  0.0 29.8 %shard_map.73 = f32[44,704]{1,0:T(8,128)} custom-call(f32[300,2816]{1,0:T(8,128)} %bitcast.2, f32[44,4800]{1,0:T(8,128)} %w_hbm.1, s32[176]{0:T(256)} %slab_hbm.1, s32[1200]{0:T(1024)} %virtual_hbm.1, s32[16]{0:T(128)} %occupied_hbm.1, f32[16]{0:T(128)} %occupied_energy_hbm.1, f32[176]{0:T(256)} %slab_energy_hbm.1), custom_call_target="tpu_custom_call" | custom-call | tf_op jit(solution)/shard_map/pallas_call | solution.py:470
  29.8 1.6 %copy.9 = f32[704,44]{0,1:T(8,128)} copy(f32[704,44]{0,1:T(8,128)} %bitcast.3) | data formatting | bytes 247808

commit v9 on v8

--- a/solution.py
+++ b/solution.py
@@ -403,7 +403,7 @@
                         o_pass.at[m],
                         o_send.at[0, X * n + m],
                         pass_recv,
-                        z_at[7] * PLACES + here + core,
+                        z_at[6] * PLACES + here + core,
                         x,
                     )
                 elif n or m or j:
@@ -422,10 +422,10 @@
     for m in range(X):
         send(
             o_pass.at[m],
-            o_got.at[z_at[1] * PLACES + 2 * x + core],
+            o_got.at[z_at[2] * PLACES + 2 * x + core],
             pass_send.at[m],
             o_recv,
-            z_at[5] * PLACES + here + core,
+            z_at[6] * PLACES + here + core,
             x_at[m],
         )
 

time: 31.5 us -> 31.5 us (level)
  no operation moved by 1% of the time
where the time goes in v9:
time: 31.5 us; the launch traced here: 31.4 us
  Pallas kernels  29.8 us (95%)
  local copies, waits for them, and re-layouts  1.58 us (5%)
    pallas_call x1, Pallas kernels, local(): pl.pallas_call(kernel, out_shape=jax.ShapeDtypeStruct((BJ, MY), F32), in_...  29.8 us
    unnamed x1, local copies, waits for them, and re-layouts  1.58 us

profile of v9, /device:TPU:1, one launch (start us, length us, event | category | flops | bytes accessed | tf_op | source)
XLA Modules:
  0.0 31.4 jit_solution(3994250876163182634)
XLA Ops:
  0.0 29.8 %shard_map.73 = f32[44,704]{1,0:T(8,128)} custom-call(f32[300,2816]{1,0:T(8,128)} %bitcast.2, f32[44,4800]{1,0:T(8,128)} %w_hbm.1, s32[176]{0:T(256)} %slab_hbm.1, s32[1200]{0:T(1024)} %virtual_hbm.1, s32[16]{0:T(128)} %occupied_hbm.1, f32[16]{0:T(128)} %occupied_energy_hbm.1, f32[176]{0:T(256)} %slab_energy_hbm.1), custom_call_target="tpu_custom_call" | custom-call | tf_op jit(solution)/shard_map/pallas_call | solution.py:470
  29.8 1.6 %copy.9 = f32[704,44]{0,1:T(8,128)} copy(f32[704,44]{0,1:T(8,128)} %bitcast.3) | data formatting | bytes 247808
